TPU v7x, 32 devices: a whole 2x2x4 slice. The times are simulated.
32 devices in a mesh: gx: 4 (over y, core), gy: 8 (over z, x).
Axes of the slice: x: 2, y: 2, z: 4, core: 2. Of those that a mesh axis runs over, the one named last changes fastest.
Arguments:
- features: bfloat16 [4096, 128], P(('gx', 'gy'))
- positions: float32 [3, 4096], P(None, ('gx', 'gy')), as said below
- wave_vectors: int32 [3, 16384], replicated, may hold values from -24 to 24, as said below
- filter_width: float32 [16], replicated, may hold values from 0.002 to 0.02
- w_charge: bfloat16 [128, 16], replicated, may hold values from -0.5 to 0.5
- w_filter_in: bfloat16 [20, 128], replicated, may hold values from -1.25 to 1.25
- filter_output_weight: bfloat16 [128, 128], replicated, may hold values from -0.5 to 0.5
- update_weight: bfloat16 [128, 128], replicated, may hold values from -0.125 to 0.125
- w_long: float32 [16, 128], replicated, may hold values from -1.5 to 1.5
- send_along_x: int32 [2, 1024], P(None, ('gx', 'gy')), may hold values from 0 to 127, as said below
- send_along_y: int32 [2, 1024], P(None, ('gx', 'gy')), may hold values from 0 to 191, as said below
- neighbours: int32 [64, 4096], P(None, ('gx', 'gy')), may hold values from 0 to 255
- neighbour_count: int32 [4096], P(('gx', 'gy')), may hold values from 8 to 64, as said below
- distances: float32 [64, 4096], P(None, ('gx', 'gy')), may hold values from 0.8 to 4.8
Outputs:
- updated: bfloat16 [4096, 128], P(('gx', 'gy'))
- forces: float32 [3, 4096], P(None, ('gx', 'gy'))
Inputs may be any that keep to these rules, and one draw needn't show every extreme that they name: `positions`: fractional coordinates; atom i lies inside the x-y cell of its domain, z below one half. `wave_vectors`: distinct integer triples with a first component of 1 to 24 and the others from -24 to 23. `send_along_x`: each list of a domain holds 32 distinct atoms of that domain. `send_along_y`: each list of a domain holds 32 distinct rows of that domain's first_table. `neighbours`: rows of the ghost table of the atom's domain; slots at or past neighbour_count are unused. `neighbour_count`: every domain has an atom with all 64 slots used.
All inputs are finite; a program needn't handle non-finite values.
Results may differ from a plain program's by a relative error of at most 0.0062.
Values may be sent and summed in bfloat16 or wider, within the bound.
No kernel may reach another device: no remote copies, remote signals or barrier semaphores. Data moves between devices by JAX's collectives and lax.ppermute only.
A program may use at most 128 MiB of HBM per device.

v0:
```python
import math

import jax
import jax.numpy as jnp
from jax import lax
from jax.sharding import PartitionSpec as P

two_pi = 2.0 * math.pi
force_unit = 0.001


def passed_along(block, axis, distance):
    devices = range(lax.axis_size(axis))
    route = [((i - distance) % len(devices), i) for i in devices]
    return lax.ppermute(block, axis, route)


def shifted_softplus(value):
    return jax.nn.softplus(value) - math.log(2.0)


def phase_table(k_piece, coords):
    kf = k_piece.astype(jnp.float32)
    angle = two_pi * (
        kf[0][:, None] * coords[0][None, :]
        + kf[1][:, None] * coords[1][None, :]
        + kf[2][:, None] * coords[2][None, :]
    )
    return jnp.stack([jnp.cos(angle), jnp.sin(angle)]).astype(jnp.bfloat16)


def filter_structure(structure, k_piece, filter_width):
    kf = k_piece.astype(jnp.float32)
    squared = two_pi * two_pi * (kf[0] * kf[0] + kf[1] * kf[1] + 0.25 * kf[2] * kf[2])
    weight = (
        jnp.exp(-0.5 * (filter_width * filter_width)[:, None] * squared[None, :])
        * (two_pi * two_pi / squared)[None, :]
    )
    return structure * weight[:, None, :]


def expand_filtered(filtered, k_piece):
    kf = k_piece.astype(jnp.float32)
    pieces = [filtered]
    for axis_index in range(3):
        factor = two_pi * kf[axis_index]
        pieces.append(jnp.stack([factor * filtered[:, 1], -factor * filtered[:, 0]], axis=1))
    return jnp.concatenate(pieces, axis=0).astype(jnp.bfloat16)


def build_coefficients(structure, k_piece, filter_width):
    return expand_filtered(filter_structure(structure, k_piece, filter_width), k_piece)


def project(coefficient_piece, k_piece, coords):
    wave_table = phase_table(k_piece, coords)
    return jnp.einsum(
        "rpk,pka->ra", coefficient_piece, wave_table, preferred_element_type=jnp.float32
    )


def per_device(
    features,
    positions,
    wave_vectors,
    filter_width,
    w_charge,
    w_filter_in,
    filter_output_weight,
    update_weight,
    w_long,
    send_along_x,
    send_along_y,
    neighbours,
    neighbour_count,
    distances,
):
    atom_rows = features.shape[0]
    channels = w_charge.shape[1]
    wave_total = wave_vectors.shape[1]
    devices = lax.axis_size("gx") * lax.axis_size("gy")
    charges = jnp.dot(features, w_charge, preferred_element_type=jnp.float32).astype(jnp.bfloat16).T
    totals = lax.psum(jnp.sum(charges.astype(jnp.float32), axis=1), ("gx", "gy"))
    mean_charge = totals / (atom_rows * devices)
    k_block = math.gcd(wave_total, 2048)
    k_turns = wave_total // k_block
    extended = jnp.concatenate([charges, jnp.ones((1, atom_rows), jnp.bfloat16)], axis=0)

    def forward(turn_index, raw):
        k_piece = lax.dynamic_slice_in_dim(wave_vectors, turn_index * k_block, k_block, 1)
        wave_table = phase_table(k_piece, positions)
        partial_sum = jnp.einsum(
            "ca,pka->cpk", extended, wave_table, preferred_element_type=jnp.float32
        )
        return lax.dynamic_update_slice_in_dim(raw, partial_sum, turn_index * k_block, 2)

    raw = lax.fori_loop(0, k_turns, forward, jnp.zeros((channels + 1, 2, wave_total), jnp.float32))
    terms = raw[:channels] - mean_charge[:, None, None] * raw[channels][None]
    summed = lax.psum(terms, ("gx", "gy"))
    empty_fields = jnp.zeros((4 * channels, atom_rows), jnp.float32)
    coefficients = build_coefficients(summed, wave_vectors, filter_width)

    def backward(turn_index, running):
        k_piece = lax.dynamic_slice_in_dim(wave_vectors, turn_index * k_block, k_block, 1)
        coefficient_piece = lax.dynamic_slice_in_dim(coefficients, turn_index * k_block, k_block, 2)
        return running + project(coefficient_piece, k_piece, positions)

    fields = lax.fori_loop(0, k_turns, backward, empty_fields)
    fields = fields * (1.0 / math.sqrt(atom_rows * devices))
    pieces = [features]
    for direction, stride in ((0, 1), (1, -1)):
        chosen = jnp.take(features, send_along_x[direction], axis=0)
        pieces.append(passed_along(chosen, "gx", stride))
    first_table = jnp.concatenate(pieces, axis=0)
    pieces = [first_table]
    for direction, stride in ((0, 1), (1, -1)):
        chosen = jnp.take(first_table, send_along_y[direction], axis=0)
        pieces.append(passed_along(chosen, "gy", stride))
    ghost_table = jnp.concatenate(pieces, axis=0)
    radial_count = w_filter_in.shape[0]
    slot_total = neighbours.shape[0]
    slot_block = math.gcd(slot_total, 16)
    centers = 5.0 * jnp.arange(radial_count, dtype=jnp.float32) / (radial_count - 1)
    sharpness = 0.02 * (radial_count - 1) * (radial_count - 1)

    def add_slots(turn_index, running):
        first_slot = turn_index * slot_block
        neighbour_ids = lax.dynamic_slice_in_dim(neighbours, first_slot, slot_block, 0)
        lengths = lax.dynamic_slice_in_dim(distances, first_slot, slot_block, 0)
        offsets = lengths[..., None] - centers
        radial_basis = jnp.exp(-sharpness * offsets * offsets).astype(jnp.bfloat16)
        hidden_features = shifted_softplus(
            jnp.einsum("sar,rf->saf", radial_basis, w_filter_in, preferred_element_type=jnp.float32)
        ).astype(jnp.bfloat16)
        filter_values = jnp.einsum(
            "saf,fg->sag", hidden_features, filter_output_weight, preferred_element_type=jnp.float32
        )
        neighbour_rows = jnp.take(ghost_table, neighbour_ids, axis=0)
        slot_ids = first_slot + lax.broadcasted_iota(jnp.int32, neighbour_ids.shape, 0)
        envelope = jnp.where(
            slot_ids < neighbour_count[None, :], 0.5 * (jnp.cos(math.pi * lengths / 5.0) + 1.0), 0.0
        )
        return running + jnp.sum(
            envelope[..., None] * neighbour_rows.astype(jnp.float32) * filter_values, axis=0
        )

    messages = lax.fori_loop(
        0,
        slot_total // slot_block,
        add_slots,
        jnp.zeros((atom_rows, features.shape[1]), jnp.float32),
    )
    messages = messages.astype(jnp.bfloat16)
    updated = features.astype(jnp.float32) + jnp.dot(
        messages, update_weight, preferred_element_type=jnp.float32
    )
    updated = updated + jnp.dot(fields[:channels].T, w_long, precision=lax.Precision.HIGHEST)
    centred = charges.astype(jnp.float32) - mean_charge[:, None]
    field_parts = fields[channels:].reshape(3, channels, atom_rows)
    forces = -force_unit * jnp.sum(centred[None] * field_parts, axis=1)
    return (updated.astype(jnp.bfloat16), forces)


def solution(mesh):
    placed = (
        P(("gx", "gy"), None),
        P(None, ("gx", "gy")),
        P(),
        P(),
        P(),
        P(),
        P(),
        P(),
        P(),
        P(None, ("gx", "gy")),
        P(None, ("gx", "gy")),
        P(None, ("gx", "gy")),
        P(("gx", "gy")),
        P(None, ("gx", "gy")),
    )
    return jax.shard_map(
        per_device,
        mesh=mesh,
        in_specs=placed,
        out_specs=(P(("gx", "gy"), None), P(None, ("gx", "gy"))),
        check_vma=False,
    )
```

profile of v0, /device:TPU:0, one launch (start us, length us, event | category | flops | bytes accessed | tf_op | source)
XLA Modules:
  0.0 306.4 jit_solution(8250279330702650680)
XLA Ops:
  8.0 1.3 gather_fusion.1
  9.9 1.3 gather_fusion.2
  11.3 2.0 collective-permute-start.1
  13.3 1.0 convert_reduce_fusion
  14.5 52.9 %while.43 = (s32[]{:T(128)}, f32[17,2,16384]{2,0,1:T(8,128)S(1)}, s32[3,16384]{1,0:T(4,128)}, f32[3,128]{1,0:T(4,128)}, bf16[17,128]{1,0:T(8,128)(2,1)S(1)}, /*index=5*/s32[]{:T(128)}, s32[]{:T(128)}, s32[]{:T(128)}, s32[]{:T(128)}) while((s32[]{:T(128)}, f32[17,2,16384]{2,0,1:T(8,128)S(1)}, s32[3,16384]{1,0:T(4,128)}, f32[3,128]{1,0:T(4,128)}, ...), condition=%wide.region_4.7_spmd, body=%wide.region_3.6_spmd.sunk | while | flops 20453380 | bytes 2624155 | solution.py:97
  16.1 4.4 %cosine_convert_fusion.4 = (bf16[1,2048,128]{2,1,0:T(8,128)(2,1)S(1)}, bf16[1,2048,128]{2,1,0:T(8,128)(2,1)S(1)}) fusion(f32[128]{0:T(128)S(1)} %get-tuple-element.675, f32[2048]{0:T(1024)S(1)} %bitcast.100, f32[128]{0:T(128)S(1)} %get-tuple-element.677, f32[2048]{0:T(1024)S(1)} %bitcast.101, f32[128]{0:T(128)S(1)} %get-tuple-element.679, ...), kind=kLoop, calls=%fused_computation.12.clone.1 | loop fusion | flops 2097152 | bytes 1074688 | tf_op jit(solution)/shard_map/convert
  22.7 4.4 %cosine_convert_fusion.4 = (bf16[1,2048,128]{2,1,0:T(8,128)(2,1)S(1)}, bf16[1,2048,128]{2,1,0:T(8,128)(2,1)S(1)}) fusion(f32[128]{0:T(128)S(1)} %get-tuple-element.675, f32[2048]{0:T(1024)S(1)} %bitcast.100, f32[128]{0:T(128)S(1)} %get-tuple-element.677, f32[2048]{0:T(1024)S(1)} %bitcast.101, f32[128]{0:T(128)S(1)} %get-tuple-element.679, ...), kind=kLoop, calls=%fused_computation.12.clone.1 | loop fusion | flops 2097152 | bytes 1074688 | tf_op jit(solution)/shard_map/convert
  29.3 4.4 %cosine_convert_fusion.4 = (bf16[1,2048,128]{2,1,0:T(8,128)(2,1)S(1)}, bf16[1,2048,128]{2,1,0:T(8,128)(2,1)S(1)}) fusion(f32[128]{0:T(128)S(1)} %get-tuple-element.675, f32[2048]{0:T(1024)S(1)} %bitcast.100, f32[128]{0:T(128)S(1)} %get-tuple-element.677, f32[2048]{0:T(1024)S(1)} %bitcast.101, f32[128]{0:T(128)S(1)} %get-tuple-element.679, ...), kind=kLoop, calls=%fused_computation.12.clone.1 | loop fusion | flops 2097152 | bytes 1074688 | tf_op jit(solution)/shard_map/convert
  36.0 4.4 %cosine_convert_fusion.4 = (bf16[1,2048,128]{2,1,0:T(8,128)(2,1)S(1)}, bf16[1,2048,128]{2,1,0:T(8,128)(2,1)S(1)}) fusion(f32[128]{0:T(128)S(1)} %get-tuple-element.675, f32[2048]{0:T(1024)S(1)} %bitcast.100, f32[128]{0:T(128)S(1)} %get-tuple-element.677, f32[2048]{0:T(1024)S(1)} %bitcast.101, f32[128]{0:T(128)S(1)} %get-tuple-element.679, ...), kind=kLoop, calls=%fused_computation.12.clone.1 | loop fusion | flops 2097152 | bytes 1074688 | tf_op jit(solution)/shard_map/convert
  42.6 4.4 %cosine_convert_fusion.4 = (bf16[1,2048,128]{2,1,0:T(8,128)(2,1)S(1)}, bf16[1,2048,128]{2,1,0:T(8,128)(2,1)S(1)}) fusion(f32[128]{0:T(128)S(1)} %get-tuple-element.675, f32[2048]{0:T(1024)S(1)} %bitcast.100, f32[128]{0:T(128)S(1)} %get-tuple-element.677, f32[2048]{0:T(1024)S(1)} %bitcast.101, f32[128]{0:T(128)S(1)} %get-tuple-element.679, ...), kind=kLoop, calls=%fused_computation.12.clone.1 | loop fusion | flops 2097152 | bytes 1074688 | tf_op jit(solution)/shard_map/convert
  49.2 4.4 %cosine_convert_fusion.4 = (bf16[1,2048,128]{2,1,0:T(8,128)(2,1)S(1)}, bf16[1,2048,128]{2,1,0:T(8,128)(2,1)S(1)}) fusion(f32[128]{0:T(128)S(1)} %get-tuple-element.675, f32[2048]{0:T(1024)S(1)} %bitcast.100, f32[128]{0:T(128)S(1)} %get-tuple-element.677, f32[2048]{0:T(1024)S(1)} %bitcast.101, f32[128]{0:T(128)S(1)} %get-tuple-element.679, ...), kind=kLoop, calls=%fused_computation.12.clone.1 | loop fusion | flops 2097152 | bytes 1074688 | tf_op jit(solution)/shard_map/convert
  55.8 4.4 %cosine_convert_fusion.4 = (bf16[1,2048,128]{2,1,0:T(8,128)(2,1)S(1)}, bf16[1,2048,128]{2,1,0:T(8,128)(2,1)S(1)}) fusion(f32[128]{0:T(128)S(1)} %get-tuple-element.675, f32[2048]{0:T(1024)S(1)} %bitcast.100, f32[128]{0:T(128)S(1)} %get-tuple-element.677, f32[2048]{0:T(1024)S(1)} %bitcast.101, f32[128]{0:T(128)S(1)} %get-tuple-element.679, ...), kind=kLoop, calls=%fused_computation.12.clone.1 | loop fusion | flops 2097152 | bytes 1074688 | tf_op jit(solution)/shard_map/convert
  62.4 4.4 %cosine_convert_fusion.4 = (bf16[1,2048,128]{2,1,0:T(8,128)(2,1)S(1)}, bf16[1,2048,128]{2,1,0:T(8,128)(2,1)S(1)}) fusion(f32[128]{0:T(128)S(1)} %get-tuple-element.675, f32[2048]{0:T(1024)S(1)} %bitcast.100, f32[128]{0:T(128)S(1)} %get-tuple-element.677, f32[2048]{0:T(1024)S(1)} %bitcast.101, f32[128]{0:T(128)S(1)} %get-tuple-element.679, ...), kind=kLoop, calls=%fused_computation.12.clone.1 | loop fusion | flops 2097152 | bytes 1074688 | tf_op jit(solution)/shard_map/convert
  68.3 41.3 %psum.14 = f32[16]{0:T(128)S(1)} all-reduce(f32[16]{0:T(128)S(1)} %get-tuple-element.555), channel_id=1, replica_groups=mesh['gx'=4,'gy'=8] {'gx','gy'}, use_global_device_ids=true, to_apply=%region_6.9 | all-reduce | flops 16 | bytes 128 | tf_op jit(solution)/shard_map/psum | solution.py:83
  110.1 2.5 multiply_subtract_fusion
  116.3 2.3 collective-permute-start.2
  119.3 2.4 collective-permute-start.3
  121.7 1.1 collective-permute-done.2
  123.1 34.5 %while.44 = (s32[]{:T(128)}, f32[128,128]{1,0:T(8,128)S(1)}, s32[128]{0:T(128)S(1)}, f32[64,128]{1,0:T(8,128)}, s32[64,128]{1,0:T(8,128)S(1)}, /*index=5*/bf16[2...) while((s32[]{:T(128)}, f32[128,128]{1,0:T(8,128)S(1)}, ...), condition=%wide.region_2.5_spmd.clone, body=%wide.region_0.4_spmd.clone.sunk | while | flops 83294248 | bytes 4114405 | solution.py:147
  123.1 6.2 %gather_fusion = bf16[2048,128]{1,0:T(8,128)(2,1)S(1)} fusion(bf16[256,128]{1,0:T(8,128)(2,1)S(1)} %get-tuple-element.737, s32[2048]{0:T(1024)S(1)} %bitcast_clamp_fusion.2), kind=kCustom, calls=%fused_computation.2.clone.clone.1 | custom fusion | bytes 1056768 | tf_op jit(solution)/shard_map/while/body/eval_jaxpr/jit(_take)/gather | solution.py:138
  130.6 1.1 fusion.64
  131.8 6.2 %gather_fusion = bf16[2048,128]{1,0:T(8,128)(2,1)S(1)} fusion(bf16[256,128]{1,0:T(8,128)(2,1)S(1)} %get-tuple-element.737, s32[2048]{0:T(1024)S(1)} %bitcast_clamp_fusion.2), kind=kCustom, calls=%fused_computation.2.clone.clone.1 | custom fusion | bytes 1056768 | tf_op jit(solution)/shard_map/while/body/eval_jaxpr/jit(_take)/gather | solution.py:138
  139.2 1.1 fusion.64
  140.4 6.2 %gather_fusion = bf16[2048,128]{1,0:T(8,128)(2,1)S(1)} fusion(bf16[256,128]{1,0:T(8,128)(2,1)S(1)} %get-tuple-element.737, s32[2048]{0:T(1024)S(1)} %bitcast_clamp_fusion.2), kind=kCustom, calls=%fused_computation.2.clone.clone.1 | custom fusion | bytes 1056768 | tf_op jit(solution)/shard_map/while/body/eval_jaxpr/jit(_take)/gather | solution.py:138
  147.8 1.1 fusion.64
  149.0 6.2 %gather_fusion = bf16[2048,128]{1,0:T(8,128)(2,1)S(1)} fusion(bf16[256,128]{1,0:T(8,128)(2,1)S(1)} %get-tuple-element.737, s32[2048]{0:T(1024)S(1)} %bitcast_clamp_fusion.2), kind=kCustom, calls=%fused_computation.2.clone.clone.1 | custom fusion | bytes 1056768 | tf_op jit(solution)/shard_map/while/body/eval_jaxpr/jit(_take)/gather | solution.py:138
  156.5 1.1 fusion.64
  157.8 88.6 %all-reduce.3.cloned.1.call-done = f32[16,2,16384]{2,0,1:T(8,128)} async-done(((f32[16,2,16384]{2,0,1:T(8,128)}), f32[16,2,16384]{2,0,1:T(8,128)}) %all-reduce.3.cloned.1.call-update) | async-done | bytes 2097168 | tf_op jit(solution)/shard_map/psum | solution.py:99
  246.4 1.8 fusion.39
  248.7 2.5 maximum_maximum_fusion
  251.3 46.7 %while.45 = (s32[]{:T(128)}, f32[64,128]{1,0:T(8,128)S(1)}, bf16[64,2,16384]{2,0,1:T(8,128)(2,1)}, s32[3,16384]{1,0:T(4,128)S(1)}, f32[3,128]{1,0:T(4,128)S(1)},...) while((s32[]{:T(128)}, f32[64,128]{1,0:T(8,128)S(1)}, bf16[64,2,16384]{2,0,1:T(8,128)(2,1)}, ...), condition=%wide.region_9.12_spmd.clone, body=%wide.region_8.0_spmd.clone.sunk | while | flops 69752840 | bytes 2814629 | solution.py:108
  251.3 4.4 %cosine_convert_fusion.5 = (bf16[1,2048,128]{2,1,0:T(8,128)(2,1)S(1)}, bf16[1,2048,128]{2,1,0:T(8,128)(2,1)S(1)}) fusion(f32[128]{0:T(128)S(1)} %get-tuple-element.700, f32[2048]{0:T(1024)S(1)} %bitcast.103, f32[128]{0:T(128)S(1)} %get-tuple-element.702, f32[2048]{0:T(1024)S(1)} %bitcast.104, f32[128]{0:T(128)S(1)} %get-tuple-element.704, ...), kind=kLoop, calls=%fused_computation.26.clone.1 | loop fusion | flops 2097152 | bytes 1074688 | tf_op jit(solution)/shard_map/convert.2
  255.7 1.4 fusion.68
  257.2 4.4 %cosine_convert_fusion.5 = (bf16[1,2048,128]{2,1,0:T(8,128)(2,1)S(1)}, bf16[1,2048,128]{2,1,0:T(8,128)(2,1)S(1)}) fusion(f32[128]{0:T(128)S(1)} %get-tuple-element.700, f32[2048]{0:T(1024)S(1)} %bitcast.103, f32[128]{0:T(128)S(1)} %get-tuple-element.702, f32[2048]{0:T(1024)S(1)} %bitcast.104, f32[128]{0:T(128)S(1)} %get-tuple-element.704, ...), kind=kLoop, calls=%fused_computation.26.clone.1 | loop fusion | flops 2097152 | bytes 1074688 | tf_op jit(solution)/shard_map/convert.2
  261.5 1.4 fusion.68
  263.0 4.4 %cosine_convert_fusion.5 = (bf16[1,2048,128]{2,1,0:T(8,128)(2,1)S(1)}, bf16[1,2048,128]{2,1,0:T(8,128)(2,1)S(1)}) fusion(f32[128]{0:T(128)S(1)} %get-tuple-element.700, f32[2048]{0:T(1024)S(1)} %bitcast.103, f32[128]{0:T(128)S(1)} %get-tuple-element.702, f32[2048]{0:T(1024)S(1)} %bitcast.104, f32[128]{0:T(128)S(1)} %get-tuple-element.704, ...), kind=kLoop, calls=%fused_computation.26.clone.1 | loop fusion | flops 2097152 | bytes 1074688 | tf_op jit(solution)/shard_map/convert.2
  267.4 1.4 fusion.68
  268.9 4.4 %cosine_convert_fusion.5 = (bf16[1,2048,128]{2,1,0:T(8,128)(2,1)S(1)}, bf16[1,2048,128]{2,1,0:T(8,128)(2,1)S(1)}) fusion(f32[128]{0:T(128)S(1)} %get-tuple-element.700, f32[2048]{0:T(1024)S(1)} %bitcast.103, f32[128]{0:T(128)S(1)} %get-tuple-element.702, f32[2048]{0:T(1024)S(1)} %bitcast.104, f32[128]{0:T(128)S(1)} %get-tuple-element.704, ...), kind=kLoop, calls=%fused_computation.26.clone.1 | loop fusion | flops 2097152 | bytes 1074688 | tf_op jit(solution)/shard_map/convert.2
  273.2 1.4 fusion.68
  274.7 4.4 %cosine_convert_fusion.5 = (bf16[1,2048,128]{2,1,0:T(8,128)(2,1)S(1)}, bf16[1,2048,128]{2,1,0:T(8,128)(2,1)S(1)}) fusion(f32[128]{0:T(128)S(1)} %get-tuple-element.700, f32[2048]{0:T(1024)S(1)} %bitcast.103, f32[128]{0:T(128)S(1)} %get-tuple-element.702, f32[2048]{0:T(1024)S(1)} %bitcast.104, f32[128]{0:T(128)S(1)} %get-tuple-element.704, ...), kind=kLoop, calls=%fused_computation.26.clone.1 | loop fusion | flops 2097152 | bytes 1074688 | tf_op jit(solution)/shard_map/convert.2
  279.1 1.4 fusion.68
  280.6 4.4 %cosine_convert_fusion.5 = (bf16[1,2048,128]{2,1,0:T(8,128)(2,1)S(1)}, bf16[1,2048,128]{2,1,0:T(8,128)(2,1)S(1)}) fusion(f32[128]{0:T(128)S(1)} %get-tuple-element.700, f32[2048]{0:T(1024)S(1)} %bitcast.103, f32[128]{0:T(128)S(1)} %get-tuple-element.702, f32[2048]{0:T(1024)S(1)} %bitcast.104, f32[128]{0:T(128)S(1)} %get-tuple-element.704, ...), kind=kLoop, calls=%fused_computation.26.clone.1 | loop fusion | flops 2097152 | bytes 1074688 | tf_op jit(solution)/shard_map/convert.2
  284.9 1.4 fusion.68
  286.4 4.4 %cosine_convert_fusion.5 = (bf16[1,2048,128]{2,1,0:T(8,128)(2,1)S(1)}, bf16[1,2048,128]{2,1,0:T(8,128)(2,1)S(1)}) fusion(f32[128]{0:T(128)S(1)} %get-tuple-element.700, f32[2048]{0:T(1024)S(1)} %bitcast.103, f32[128]{0:T(128)S(1)} %get-tuple-element.702, f32[2048]{0:T(1024)S(1)} %bitcast.104, f32[128]{0:T(128)S(1)} %get-tuple-element.704, ...), kind=kLoop, calls=%fused_computation.26.clone.1 | loop fusion | flops 2097152 | bytes 1074688 | tf_op jit(solution)/shard_map/convert.2
  290.8 1.4 fusion.68
  292.3 4.4 %cosine_convert_fusion.5 = (bf16[1,2048,128]{2,1,0:T(8,128)(2,1)S(1)}, bf16[1,2048,128]{2,1,0:T(8,128)(2,1)S(1)}) fusion(f32[128]{0:T(128)S(1)} %get-tuple-element.700, f32[2048]{0:T(1024)S(1)} %bitcast.103, f32[128]{0:T(128)S(1)} %get-tuple-element.702, f32[2048]{0:T(1024)S(1)} %bitcast.104, f32[128]{0:T(128)S(1)} %get-tuple-element.704, ...), kind=kLoop, calls=%fused_computation.26.clone.1 | loop fusion | flops 2097152 | bytes 1074688 | tf_op jit(solution)/shard_map/convert.2
  296.6 1.4 fusion.68
  298.7 0.9 fusion.31
  (145 shorter events, 32.1 us)
Async XLA Ops:
  7.2 150.5 %copy-start = (bf16[128,128]{1,0:T(8,128)(2,1)S(1)}, bf16[128,128]{1,0:T(8,128)(2,1)}, u32[]{:S(2)}) copy-start(bf16[128,128]{1,0:T(8,128)(2,1)} %param.31) | copy-start | bytes 98308
  7.2 239.3 %all-reduce.3.cloned.1.call-start = ((), (), s32[]{:S(2)}) async-start(), calls=%async_computation | async-start | bytes 4194304 | tf_op jit(solution)/shard_map/psum | solution.py:99
  9.4 106.2 %collective-permute-start = (bf16[32,128]{1,0:T(8,128)(2,1)S(1)}, bf16[32,128]{1,0:T(8,128)(2,1)S(1)}, u32[]{:S(2)}, u32[]{:S(2)}) collective-permute-start(bf16[32,128]{1,0:T(8,128)(2,1)S(1)} %broadcast_select_fusion.3), channel_id=1, source_target_pairs={{24,0},{0,8},{8,16},{16,24},{25,1},{1,9},{9,17},{17,25},{26,2},{2,... | collective-permute-start | bytes 24584 | tf_op jit(solution)/shard_map/ppermute | solution.py:15
  11.3 104.3 %collective-permute-start.1 = (bf16[32,128]{1,0:T(8,128)(2,1)S(1)}, bf16[32,128]{1,0:T(8,128)(2,1)S(1)}, u32[]{:S(2)}, u32[]{:S(2)}) collective-permute-start(bf16[32,128]{1,0:T(8,128)(2,1)S(1)} %broadcast_select_fusion.2), channel_id=1, source_target_pairs={{8,0},{16,8},{24,16},{0,24},{9,1},{17,9},{25,17},{1,25},{10,2},{18... | collective-permute-start | bytes 24584 | tf_op jit(solution)/shard_map/ppermute | solution.py:15
  67.4 45.2 %copy-start.1 = (bf16[128,128]{1,0:T(8,128)(2,1)S(1)}, bf16[128,128]{1,0:T(8,128)(2,1)}, u32[]{:S(2)}) copy-start(bf16[128,128]{1,0:T(8,128)(2,1)} %param.24) | copy-start | bytes 98308
  67.4 45.2 %copy-start.2 = (s32[3,16384]{1,0:T(4,128)S(1)}, s32[3,16384]{1,0:T(4,128)}, u32[]{:S(2)}) copy-start(s32[3,16384]{1,0:T(4,128)} %get-tuple-element.802) | copy-start | bytes 589828
  109.6 0.5 copy-start.8
  110.1 13.0 %copy-start.3 = (s32[64,128]{1,0:T(8,128)S(1)}, s32[64,128]{1,0:T(8,128)}, u32[]{:S(2)}) copy-start(s32[64,128]{1,0:T(8,128)} %param.35) | copy-start | bytes 98308
  110.1 13.0 %copy-start.4 = (bf16[20,128]{1,0:T(8,128)(2,1)S(1)}, bf16[20,128]{1,0:T(8,128)(2,1)}, u32[]{:S(2)}) copy-start(bf16[20,128]{1,0:T(8,128)(2,1)} %param.29) | copy-start | bytes 15364
  110.1 13.0 %copy-start.6 = (s32[128]{0:T(128)S(1)}, s32[128]{0:T(128)}, u32[]{:S(2)}) copy-start(s32[128]{0:T(128)} %param.36) | copy-start | bytes 1540
  112.6 10.5 %copy-start.9 = (bf16[128,128]{1,0:T(8,128)(2,1)S(1)}, bf16[128,128]{1,0:T(8,128)(2,1)}, u32[]{:S(2)}) copy-start(bf16[128,128]{1,0:T(8,128)(2,1)} %param.30) | copy-start | bytes 98308
  116.3 6.5 %collective-permute-start.2 = (bf16[32,128]{1,0:T(8,128)(2,1)S(1)}, bf16[32,128]{1,0:T(8,128)(2,1)S(1)}, u32[]{:S(2)}, u32[]{:S(2)}) collective-permute-start(bf16[32,128]{1,0:T(8,128)(2,1)S(1)} %broadcast_select_fusion.1), channel_id=1, source_target_pairs={{7,0},{0,1},{1,2},{2,3},{3,4},{4,5},{5,6},{6,7},{15,8},{8,9},{9,10... | collective-permute-start | bytes 24584 | tf_op jit(solution)/shard_map/ppermute | solution.py:15
  119.3 3.8 %collective-permute-start.3 = (bf16[32,128]{1,0:T(8,128)(2,1)S(1)}, bf16[32,128]{1,0:T(8,128)(2,1)S(1)}, u32[]{:S(2)}, u32[]{:S(2)}) collective-permute-start(bf16[32,128]{1,0:T(8,128)(2,1)S(1)} %broadcast_select_fusion), channel_id=1, source_target_pairs={{1,0},{2,1},{3,2},{4,3},{5,4},{6,5},{7,6},{0,7},{9,8},{10,9},{11,1... | collective-permute-start | bytes 24584 | tf_op jit(solution)/shard_map/ppermute | solution.py:15
  248.7 2.5 copy-start.5
  251.3 47.4 %copy-start.7 = (f32[16,128]{1,0:T(8,128)S(1)}, f32[16,128]{1,0:T(8,128)}, u32[]{:S(2)}) copy-start(f32[16,128]{1,0:T(8,128)} %param.32) | copy-start | bytes 24580
Sparse Core Ops, SparseCore 0:
  112.7 133.6 all-reduce.2
where the time goes:
time: 308 us; the launch traced here: 306 us
  other arithmetic  91.1 us (30%)
  waiting for transfers between devices  90 us (29%)
  blocking collectives  41.3 us (13%)
  local copies, waits for them, and re-layouts  37.1 us (12%)
  matrix products  24.6 us (8%)
  between operations  14.2 us (5%)
  starting transfers between devices  7.18 us (2%)
    psum x1, waiting for transfers between devices, per_device(): summed = lax.psum(terms, ('gx', 'gy'))  88.6 us
    another operation x18, other arithmetic  72 us
    psum x1, blocking collectives, per_device(): lax.psum(jnp.sum(charges.astype(jnp.float32), axis=1), ('gx', 'gy'))  41.3 us
    gather x4, local copies, waits for them, and re-layouts, add_slots(): neighbour_rows = jnp.take(ghost_table, neighbour_ids, axis=0)  24.7 us
    dot_general x8, matrix products, project(): jnp.einsum('rpk,pka->ra', coefficient_piece, wave_table, preferred_elemen...  11.1 us
    ppermute x4, starting transfers between devices, passed_along(): return lax.ppermute(block, axis, route)  7.14 us
    mul x16, local copies, waits for them, and re-layouts, phase_table(): kf[0][:, None] * coords[0][None, :] + kf[1][:, None] * coords[1][None, :]  6.52 us
    convert_element_type x16, other arithmetic, phase_table(): kf = k_piece.astype(jnp.float32)  6.22 us
  transfers between devices with their start and end apart: 5, of which 3 were waited for; matrix products, arithmetic and copies ran while one was open for 32% of the time, Pallas kernels for 0%

commit v1 on v0

v1 whole, which is shorter than its diff:
```python
import math

import jax
import jax.numpy as jnp
from jax import lax
from jax.experimental import pallas as pl
from jax.experimental.pallas import tpu as pltpu
from jax.sharding import PartitionSpec as P

two_pi = 2.0 * math.pi
force_unit = 0.001
f32 = jnp.float32
bf16 = jnp.bfloat16

sin_terms = (4.442867902992535, -7.307443419719773, 3.594788063370906, -0.7843739903522723)
cos_terms = (1.414204080647301, -6.977642060724434, 5.715238411759286, -1.7283486673792663)

cos_scale = sin_terms[3] * sin_terms[3]
sin_scale = sin_terms[3] * cos_terms[3]

rounder = 1.5 * 2.0**23

payload_rows = 24
part_rows = ((0, 3), (3, 3), (6, 2))
result_rows = 24


def dot(a, b, contract, precision=None):
    return lax.dot_general(
        a, b, (contract, ((), ())), preferred_element_type=f32, precision=precision
    )


def passed_along(block, axis, distance):
    devices = range(lax.axis_size(axis))
    route = [((i - distance) % len(devices), i) for i in devices]
    return lax.ppermute(block, axis, route)


def place():
    return lax.axis_index("gx") * lax.axis_size("gy") + lax.axis_index("gy")


def over_devices(blocks):
    return lax.all_to_all(blocks, ("gx", "gy"), 0, 0, tiled=True)


def waves_of(turns):
    part = turns - ((turns + rounder) - rounder)
    square = part * part
    sine = part * polynomial(sin_terms, square)
    cosine = polynomial(cos_terms, square)
    return 1.0 / cos_scale - sine * sine, sine * cosine


def polynomial(terms, square):
    value = square + terms[2] / terms[3]
    for term in terms[1::-1]:
        value = value * square + term / terms[3]
    return value


def picked(list_row, tables):
    total, first = None, 0
    for table in tables:
        rows = table.shape[0]
        ids = lax.broadcasted_iota(jnp.int32, (rows, list_row.shape[1]), 0) + first
        chosen = jnp.where(ids == list_row, 1.0, 0.0).astype(bf16)
        part = dot(chosen, table, ((0,), (0,)))
        total = part if total is None else total + part
        first += rows
    return total


def fetched(given, held, semaphores):
    moves = [
        pltpu.make_async_copy(source, target, semaphores.at[i]) for i, (source, target) in enumerate(zip(given, held))
    ]
    for move in moves:
        move.start()
    for move in moves:
        move.wait()


def hold_kernel(*refs):
    count = (len(refs) - 1) // 2
    fetched(refs[:count], refs[count:-1], refs[-1])


def send_kernel(*refs):
    given, (copies_ref, minus_ref, plus_ref) = refs[:4], refs[4:7]
    held, rows_ref, semaphores = refs[7:11], refs[11], refs[12]
    fetched(given, held, semaphores)
    features_ref, positions_ref, w_charge_ref, lists_ref = held
    features = features_ref[...]
    channels = w_charge_ref.shape[0]
    charges = dot(w_charge_ref[...], features, ((1,), (1,))).astype(bf16).astype(f32)
    rows_ref[...] = jnp.zeros_like(rows_ref)
    rows_ref[0:channels, :] = charges
    left = positions_ref[...]
    for first, rows in part_rows:
        rounded = left.astype(bf16).astype(f32)
        rows_ref[channels + first : channels + first + rows, :] = rounded[:rows]
        left = left - rounded
    block = rows_ref[...].astype(bf16)

    def place(index, unused):
        copies_ref[index] = block
        return unused

    lax.fori_loop(0, copies_ref.shape[0], place, 0, unroll=8)
    minus_ref[...] = picked(lists_ref[0:1, :], [features]).astype(bf16)
    plus_ref[...] = picked(lists_ref[1:2, :], [features]).astype(bf16)


def second_send_kernel(features_ref, from_minus_ref, from_plus_ref, lists_ref, minus_ref, plus_ref):
    tables = [features_ref[...], from_minus_ref[...], from_plus_ref[...]]
    for direction, result_ref in enumerate((minus_ref, plus_ref)):
        result_ref[...] = picked(lists_ref[direction : direction + 1, :], tables).astype(bf16)


def factors_kernel(channels, vectors_ref, width_ref, integers_ref, factors_ref, held_ref, held_width_ref, semaphores):
    count = integers_ref.shape[0]
    window = held_ref.shape[1]
    offset = place() * count
    first = pl.multiple_of(offset // window * window, window)
    fetched((vectors_ref.at[:, pl.ds(first, window)], width_ref), (held_ref, held_width_ref), semaphores)
    vectors = held_ref[...].astype(f32)
    if window > count:
        vectors = pltpu.roll(vectors, lax.rem(window - (offset - first), window), 1)[:, :count]
    kx, ky, kz = vectors[0:1], vectors[1:2], vectors[2:3]
    squared = two_pi * two_pi * (kx * kx + ky * ky + 0.25 * kz * kz)
    diagonal = lax.broadcasted_iota(jnp.int32, (channels, channels), 0) == lax.broadcasted_iota(
        jnp.int32, (channels, channels), 1
    )
    width = jnp.sum(jnp.where(diagonal, held_width_ref[...], 0.0), axis=1, keepdims=True)
    weight = jnp.exp(-0.5 * (width * width) * squared) * (two_pi * two_pi / squared)
    factors_ref[...] = jnp.concatenate([weight] + [two_pi * along * weight for along in (kx, ky, kz)], axis=0)
    component = lax.broadcasted_iota(jnp.int32, (payload_rows, count), 0) - channels
    inside = (component >= 0) & (component < 8)
    component = lax.rem(jnp.maximum(component, 0), 3)
    integers = jnp.where(component == 0, kx, jnp.where(component == 1, ky, kz))
    integers_ref[...] = jnp.where(inside, integers, 0.0).T.astype(bf16)


per_tile = 4


def tile_of(blocks_ref, index):
    return jnp.concatenate([blocks_ref[per_tile * index + i] for i in range(per_tile)], axis=1)


def add_waves(channels, blocks_ref, integers_ref, waves_ref, joined_ref, weights_ref, turns_ref):
    devices, rows, own = blocks_ref.shape
    count = integers_ref.shape[0]
    chunk = min(count, 128)
    weights_ref[channels : 2 * channels, :] = jnp.ones((channels, devices * own), bf16)
    weights_ref[2 * channels :, :] = jnp.zeros((128 - 2 * channels, devices * own), bf16)

    def join(index, unused):
        lanes = pl.ds(pl.multiple_of(index * own, own), own)
        block = blocks_ref[index]
        joined_ref[:, lanes] = block
        weights_ref[0:channels, lanes] = block[:channels]
        return unused

    lax.fori_loop(0, devices, join, 0, unroll=8)
    turns_ref[...] = dot(integers_ref[...], joined_ref[...], ((1,), (0,)))

    def step(index, unused):
        for part in range(2):
            lanes = pl.ds(pl.multiple_of((2 * index + part) * own, own), own)
            for first in range(0, count, chunk):
                cosine, sine = waves_of(turns_ref[first : first + chunk, lanes])
                waves_ref[first : first + chunk, lanes] = cosine.astype(bf16)
                waves_ref[count + first : count + first + chunk, lanes] = sine.astype(bf16)
        return unused

    lax.fori_loop(0, devices // 2, step, 0)
    return [
        dot(waves_ref[wave * count : (wave + 1) * count, :], weights_ref[...], ((1,), (1,))) for wave in range(2)
    ]


def put_fields(channels, atoms, blocks_ref, waves_ref, coefficients_ref, mean, result_ref):
    devices, _, own = blocks_ref.shape
    count = coefficients_ref.shape[2]
    wide = per_tile * own
    scale = 1.0 / math.sqrt(atoms)

    def waves_at(index, wave):
        lanes = pl.ds(pl.multiple_of(index * wide, wide), wide)
        return waves_ref[wave * count : (wave + 1) * count, lanes]

    def step(turn, unused):
        indices = (2 * turn, 2 * turn + 1)
        fields_of = [
            sum(dot(coefficients_ref[wave], waves_at(index, wave), ((1,), (0,))) for wave in range(2))
            for index in indices
        ]
        for index, fields in zip(indices, fields_of):
            fields = fields * scale
            centred = tile_of(blocks_ref, index)[:channels].astype(f32) - mean
            rows = [fields[:channels]]
            for axis in range(3):
                along = fields[(axis + 1) * channels : (axis + 2) * channels]
                rows.append(-force_unit * jnp.sum(centred * along, axis=0, keepdims=True))
            rows.append(jnp.zeros((result_rows - channels - 3, wide), f32))
            result = jnp.concatenate(rows, axis=0)
            for i in range(per_tile):
                result_ref[per_tile * index + i] = result[:, i * own : (i + 1) * own].astype(result_ref.dtype)
        return unused

    lax.fori_loop(0, devices // (2 * per_tile), step, 0)


def waves_kernel(channels, gathered_ref, integers_ref, factors_ref, result_ref, waves_ref, coefficients_ref, *scratch):
    devices, _, own = gathered_ref.shape
    atoms = devices * own
    sums = [total.T for total in add_waves(channels, gathered_ref, integers_ref, waves_ref, *scratch)]

    def add_up(index, total):
        return total + gathered_ref[index][:channels].astype(f32)

    total = lax.fori_loop(0, devices, add_up, jnp.zeros((channels, own), f32), unroll=8)
    mean = jnp.sum(total, axis=1, keepdims=True) * (1.0 / atoms)
    cosine, sine = [total[0:channels, :] - mean * total[channels : channels + 1, :] for total in sums]
    cosine, sine = cosine * cos_scale, sine * sin_scale
    factors = factors_ref[...]
    coefficients_ref[0] = (cos_scale * factors * jnp.concatenate([cosine] + [sine] * 3, axis=0)).astype(bf16)
    coefficients_ref[1] = (sin_scale * factors * jnp.concatenate([sine] + [-cosine] * 3, axis=0)).astype(bf16)
    put_fields(channels, atoms, gathered_ref, waves_ref, coefficients_ref, mean, result_ref)


filter_group = 32


def filters_kernel(count_ref, distances_ref, w_in_ref, w_out_ref, filters_ref, radial_ref, envelope_ref):
    slots, own = distances_ref.shape
    radial = w_in_ref.shape[0]
    radial_ref[...] = jnp.zeros_like(radial_ref)
    radial_ref[0:radial, :] = w_in_ref[...].astype(f32)
    w_in = radial_ref[...].T.astype(bf16)
    w_out = w_out_ref[...].astype(f32).T.astype(bf16)
    padded = radial_ref.shape[0]
    centers = 5.0 * lax.broadcasted_iota(jnp.int32, (padded, own), 0).astype(f32) / (radial - 1)
    sharpness = 0.02 * (radial - 1) * (radial - 1)
    live = lax.broadcasted_iota(jnp.int32, (slots, own), 0) < count_ref[...]
    envelope_ref[...] = jnp.where(live, 0.5 * (cos_scale * waves_of(0.1 * distances_ref[...])[0] + 1.0), 0.0)
    pairs = range(0, filter_group, 2)

    def step(turn, unused):
        start = pl.multiple_of(turn * filter_group, filter_group)
        lengths = distances_ref[pl.ds(start, filter_group), :]
        envelope = envelope_ref[pl.ds(start, filter_group), :]
        values, filters = [], []
        for pair in pairs:
            basis = []
            for slot in (pair, pair + 1):
                offsets = lengths[slot : slot + 1] - centers
                basis.append(jnp.exp(-sharpness * offsets * offsets).astype(bf16))
            values.append(dot(w_in, jnp.concatenate(basis, axis=1), ((1,), (0,))))
        for value in values:
            hidden = (jnp.log(1.0 + jnp.exp(value)) - math.log(2.0)).astype(bf16)
            filters.append(dot(w_out, hidden, ((1,), (0,))))
        for slot in range(filter_group):
            lanes = slice(slot % 2 * own, (slot % 2 + 1) * own)
            filters_ref[start + slot] = envelope[slot : slot + 1] * filters[slot // 2][:, lanes]
        return unused

    lax.fori_loop(0, slots // filter_group, step, 0)


def messages_kernel(
    features_ref, x_minus_ref, x_plus_ref, y_minus_ref, y_plus_ref, neighbours_ref, filters_ref, w_update_ref,
    result_ref, table_ref,
):
    slots, own = neighbours_ref.shape
    width = features_ref.shape[1]
    first = 0
    for part in (features_ref, x_minus_ref, x_plus_ref, y_minus_ref, y_plus_ref):
        table_ref[first : first + part.shape[0], :] = part[...].astype(f32)
        first += part.shape[0]
    table = table_ref[...].T.astype(bf16)
    row_ids = lax.broadcasted_iota(jnp.int32, (first, own), 0).astype(f32).astype(bf16)
    ones, zeros = jnp.ones((first, own), bf16), jnp.zeros((first, own), bf16)

    ids = neighbours_ref[...].astype(f32)
    rows = []
    for pair in range(0, slots, 2):
        chosen = []
        for slot in (pair, pair + 1):
            wanted = jnp.broadcast_to(ids[slot : slot + 1], (16, own)).astype(bf16)
            wanted = jnp.concatenate([wanted] * (first // 16), axis=0)
            chosen.append(jnp.where(row_ids == wanted, ones, zeros))
        rows.append(dot(table, jnp.concatenate(chosen, axis=1), ((1,), (0,))))
    total = jnp.zeros((width, own), f32)
    for slot in range(slots):
        lanes = slice(slot % 2 * own, (slot % 2 + 1) * own)
        total = total + rows[slot // 2][:, lanes] * filters_ref[slot]
    update = dot(total.T.astype(bf16), w_update_ref[...], ((1,), (0,)))
    result_ref[...] = features_ref[...].astype(f32) + update


def final_kernel(channels, base_ref, summed_ref, w_long_ref, updated_ref, forces_ref):
    summed = jnp.sum(summed_ref[...].astype(f32), axis=0)
    potentials = summed[:channels].T
    long_range = dot(potentials, w_long_ref[...], ((1,), (0,)), lax.Precision.HIGHEST)
    updated_ref[...] = (base_ref[...] + long_range).astype(bf16)
    forces_ref[...] = summed[channels : channels + 3]


def per_device(
    features, positions, wave_vectors, filter_width, w_charge, w_filter_in, filter_output_weight,
    update_weight, w_long, send_along_x, send_along_y, neighbours, neighbour_count, distances,
):
    own, width = features.shape
    channels = w_charge.shape[1]
    devices = lax.axis_size("gx") * lax.axis_size("gy")
    count = wave_vectors.shape[1] // devices
    ghosts = send_along_x.shape[1]
    struct = jax.ShapeDtypeStruct
    small = pltpu.CompilerParams(vmem_limit_bytes=24 * 1024 * 1024)

    copies, x_minus, x_plus = pl.pallas_call(
        send_kernel,
        out_shape=(
            struct((devices, payload_rows, own), bf16), struct((ghosts, width), bf16), struct((ghosts, width), bf16),
        ),
        in_specs=[pl.BlockSpec(memory_space=pltpu.HBM)] * 4,
        scratch_shapes=[
            pltpu.VMEM((own, width), bf16),
            pltpu.VMEM((3, own), f32),
            pltpu.VMEM((channels, width), bf16),
            pltpu.VMEM(send_along_x.shape, jnp.int32),
            pltpu.VMEM((payload_rows, own), f32),
            pltpu.SemaphoreType.DMA((4,)),
        ],
        compiler_params=small,
        name="send",
    )(*[
        pltpu.with_memory_space_constraint(array, pltpu.HBM)
        for array in (features, positions, w_charge.T, send_along_x)
    ])

    x_minus = passed_along(x_minus, "gx", 1)
    x_plus = passed_along(x_plus, "gx", -1)
    integers, factors = pl.pallas_call(
        lambda *refs: factors_kernel(channels, *refs),
        out_shape=(struct((count, payload_rows), bf16), struct((4 * channels, count), f32)),
        in_specs=[pl.BlockSpec(memory_space=pltpu.HBM)] * 2,
        scratch_shapes=[
            pltpu.VMEM((wave_vectors.shape[0], max(count, 128)), jnp.int32),
            pltpu.VMEM((1, channels), f32),
            pltpu.SemaphoreType.DMA((2,)),
        ],
        compiler_params=small,
        name="factors",
    )(*[pltpu.with_memory_space_constraint(array, pltpu.HBM) for array in (wave_vectors, filter_width[None, :])])

    later = (
        features, send_along_y, neighbours, neighbour_count[None, :], distances,
        w_filter_in, filter_output_weight, update_weight, w_long,
    )
    later = pl.pallas_call(
        hold_kernel,
        out_shape=tuple(struct(array.shape, array.dtype) for array in later),
        in_specs=[pl.BlockSpec(memory_space=pltpu.HBM)] * len(later),
        scratch_shapes=[pltpu.SemaphoreType.DMA((len(later),))],
        compiler_params=small,
        name="hold",
    )(*[pltpu.with_memory_space_constraint(array, pltpu.HBM) for array in later])
    gathered, x_minus, x_plus, integers, factors, later = lax.optimization_barrier(
        (over_devices(copies), x_minus, x_plus, integers, factors, later)
    )
    (
        features, send_along_y, neighbours, neighbour_count, distances,
        w_filter_in, filter_output_weight, update_weight, w_long,
    ) = later
    held_bytes = devices * own * (8 * count + 2 * (128 + 2 * payload_rows + result_rows))
    partial = pl.pallas_call(
        lambda *refs: waves_kernel(channels, *refs),
        out_shape=struct((devices, result_rows, own), bf16),
        scratch_shapes=[
            pltpu.VMEM((2 * count, devices * own), bf16),
            pltpu.VMEM((2, 4 * channels, count), bf16),
            pltpu.VMEM((payload_rows, devices * own), bf16),
            pltpu.VMEM((128, devices * own), bf16),
            pltpu.VMEM((count, devices * own), f32),
        ],
        compiler_params=pltpu.CompilerParams(vmem_limit_bytes=held_bytes + 8 * 1024 * 1024),
        cost_estimate=pl.CostEstimate(flops=40 * count * devices * own, bytes_accessed=1 << 20, transcendentals=0),
        name="waves",
    )(gathered, integers, factors)
    partial, x_minus, x_plus = lax.optimization_barrier((partial, x_minus, x_plus))
    received = over_devices(partial)

    y_minus, y_plus = pl.pallas_call(
        second_send_kernel,
        out_shape=(struct((ghosts, width), bf16), struct((ghosts, width), bf16)),
        compiler_params=small,
        name="second_send",
    )(features, x_minus, x_plus, send_along_y)
    y_minus = passed_along(y_minus, "gy", 1)
    y_plus = passed_along(y_plus, "gy", -1)
    slots = neighbours.shape[0]
    distances, w_filter_in, x_minus = lax.optimization_barrier((distances, w_filter_in, x_minus))
    filters = pl.pallas_call(
        filters_kernel,
        out_shape=struct((slots, width, own), f32),
        scratch_shapes=[pltpu.VMEM((32, width), f32), pltpu.VMEM(distances.shape, f32)],
        compiler_params=small,
        cost_estimate=pl.CostEstimate(
            flops=2 * slots * own * width * width, bytes_accessed=1 << 20, transcendentals=2 * slots * own * width
        ),
        name="filters",
    )(neighbour_count, distances, w_filter_in, filter_output_weight)
    filters, y_minus, y_plus = lax.optimization_barrier((filters, y_minus, y_plus))
    base = pl.pallas_call(
        messages_kernel,
        out_shape=struct((own, width), f32),
        scratch_shapes=[pltpu.VMEM((own + 4 * ghosts, width), f32)],
        compiler_params=small,
        cost_estimate=pl.CostEstimate(
            flops=2 * slots * own * width * 256, bytes_accessed=1 << 20, transcendentals=0
        ),
        name="messages",
    )(features, x_minus, x_plus, y_minus, y_plus, neighbours, filters, update_weight)

    updated, forces = pl.pallas_call(
        lambda *refs: final_kernel(channels, *refs),
        out_shape=(struct((own, width), bf16), struct((3, own), f32)),
        compiler_params=small,
        name="final",
    )(base, received, w_long)
    return updated, forces


def solution(mesh):
    placed = (
        P(("gx", "gy"), None),
        P(None, ("gx", "gy")),
        P(),
        P(),
        P(),
        P(),
        P(),
        P(),
        P(),
        P(None, ("gx", "gy")),
        P(None, ("gx", "gy")),
        P(None, ("gx", "gy")),
        P(("gx", "gy")),
        P(None, ("gx", "gy")),
    )
    return jax.shard_map(
        per_device,
        mesh=mesh,
        in_specs=placed,
        out_specs=(P(("gx", "gy"), None), P(None, ("gx", "gy"))),
        check_vma=False,
    )
```

time: 308 us -> 45 us (0.15)
  other arithmetic: 91.1 us -> 0 us
  waiting for transfers between devices: 90 us -> 6.63 us
  blocking collectives: 41.3 us -> 0 us
  local copies, waits for them, and re-layouts: 37.1 us -> 0 us
  matrix products: 24.6 us -> 0 us
  Pallas kernels: 0 us -> 20.4 us
  between operations: 14.2 us -> 0.7 us
  starting transfers between devices: 7.18 us -> 16.9 us
    psum x1 -> x0, waiting for transfers between devices: 88.6 us -> none  [per_device(): summed = lax.psum(terms, ('gx', 'gy'))]
    another operation x18 -> x0, other arithmetic: 72 us -> none
    psum x1 -> x0, blocking collectives: 41.3 us -> none  [per_device(): lax.psum(jnp.sum(charges.astype(jnp.float32), axis=1), ('gx', 'gy'))]
    gather x8 -> x0, local copies, waits for them, and re-layouts: 28.6 us -> none  [the longest x4 24.7 us: add_slots(): neighbour_rows = jnp.take(ghost_table, neighbour_ids, axis=0)]
    dot_general x27 -> x0, matrix products: 24.6 us -> none  [the longest x8 11.1 us: project(): jnp.einsum('rpk,pka->ra', coefficient_piece, wave_table, preferred_elemen...]
    pallas_call x0 -> x8, Pallas kernels: none -> 20.4 us  [the longest x1 12.6 us: per_device(): pl.pallas_call(lambda *refs: waves_kernel(channels, *refs), out_shape=str...]
    all_to_all x0 -> x2, starting transfers between devices: none -> 10.4 us  [over_devices(): return lax.all_to_all(blocks, ('gx', 'gy'), 0, 0, tiled=True)]
    mul x16 -> x0, local copies, waits for them, and re-layouts: 6.52 us -> none  [phase_table(): kf[0][:, None] * coords[0][None, :] + kf[1][:, None] * coords[1][None, :]]
  transfers between devices with their start and end apart: 5 -> 6, of which waited for: 3 -> 2; matrix products, arithmetic and copies ran while one was open for 32% -> 0% of each run, Pallas kernels for 0% -> 12%
where the time goes in v1:
time: 45 us; the launch traced here: 44.6 us
  Pallas kernels  20.4 us (45%)
  starting transfers between devices  16.9 us (38%)
  waiting for transfers between devices  6.63 us (15%)
  between operations  0.7 us (2%)
    pallas_call x1, Pallas kernels, per_device(): pl.pallas_call(lambda *refs: waves_kernel(channels, *refs), out_shape=str...  12.6 us
    all_to_all x2, starting transfers between devices, over_devices(): return lax.all_to_all(blocks, ('gx', 'gy'), 0, 0, tiled=True)  10.4 us
    ppermute x4, starting transfers between devices, passed_along(): return lax.ppermute(block, axis, route)  6.54 us
    all_to_all x2, waiting for transfers between devices, over_devices(): return lax.all_to_all(blocks, ('gx', 'gy'), 0, 0, tiled=True)  4.91 us
    pallas_call x1, Pallas kernels, per_device(): pl.pallas_call(filters_kernel, out_shape=struct((slots, width, own), f32)...  2.32 us
    ppermute x4, waiting for transfers between devices, passed_along(): return lax.ppermute(block, axis, route)  1.72 us
    pallas_call x1, Pallas kernels, per_device(): pl.pallas_call(send_kernel, out_shape=(struct((devices, payload_rows, own...  1.65 us
    pallas_call x1, Pallas kernels, per_device(): pl.pallas_call(hold_kernel, out_shape=tuple((struct(array.shape, array.dt...  0.96 us
  transfers between devices with their start and end apart: 6, of which 2 were waited for; matrix products, arithmetic and copies ran while one was open for 0% of the time, Pallas kernels for 12%

profile of v1, /device:TPU:0, one launch (start us, length us, event | category | flops | bytes accessed | tf_op | source)
XLA Modules:
  0.0 44.6 jit_solution(8433630967840823521)
XLA Ops:
  0.6 1.7 %send.1 = (bf16[32,24,128]{2,1,0:T(8,128)(2,1)}, bf16[32,128]{1,0:T(8,128)(2,1)S(1)}, bf16[32,128]{1,0:T(8,128)(2,1)S(1)}) custom-call(bf16[128,128]{1,0:T(8,128)(2,1)} %refs_0_.5, f32[3,128]{1,0:T(4,128)} %refs_1_.2, bf16[16,128]{1,0:T(8,128)(2,1)} %bitcast.3, s32[2,32]{1,0:T(2,128)} %refs_3_.1), custom_call_target="tpu_custom_call" | custom-call | tf_op jit(solution)/shard_map/send/pallas_call | solution.py:325
  2.3 7.3 %all-to-all-start = ((bf16[32,24,128]{2,1,0:T(8,128)(2,1)}), bf16[32,24,128]{2,1,0:T(8,128)(2,1)S(1)}, u32[]{:S(2)}, u32[]{:S(2)}) async-start(bf16[32,24,128]{2,1,0:T(8,128)(2,1)} %get-tuple-element.41), calls=%async_computation | async-start | bytes 393216 | tf_op jit(solution)/shard_map/all_to_all | solution.py:45
  9.6 0.3 collective-permute-start
  9.9 1.5 %collective-permute-start.1 = (bf16[32,128]{1,0:T(8,128)(2,1)S(1)}, bf16[32,128]{1,0:T(8,128)(2,1)S(1)}, u32[]{:S(2)}, u32[]{:S(2)}) collective-permute-start(bf16[32,128]{1,0:T(8,128)(2,1)S(1)} %get-tuple-element.43), channel_id=1, source_target_pairs={{8,0},{16,8},{24,16},{0,24},{9,1},{17,9},{25,17},{1,25},{10,2},{18... | collective-permute-start | bytes 24584 | tf_op jit(solution)/shard_map/ppermute | solution.py:37
  11.4 0.8 %factors.1 = (bf16[512,24]{1,0:T(8,128)(2,1)S(1)}, f32[64,512]{1,0:T(8,128)S(1)}) custom-call(s32[3,16384]{1,0:T(4,128)} %refs_0_.4, f32[1,16]{1,0:T(1,128)} %bitcast.4), custom_call_target="tpu_custom_call" | custom-call | tf_op jit(solution)/shard_map/factors/pallas_call | solution.py:348
  12.3 1.0 %hold.1 = (bf16[128,128]{1,0:T(8,128)(2,1)S(1)}, s32[2,32]{1,0:T(2,128)S(1)}, s32[64,128]{1,0:T(8,128)S(1)}, s32[1,128]{1,0:T(1,128)S(1)}, f32[64,128]{1,0:T(8,1...) custom-call(bf16[128,128]{1,0:T(8,128)(2,1)} %refs_0_.5, ...), custom_call_target="tpu_custom_call" | custom-call | tf_op jit(solution)/shard_map/hold/pallas_call | solution.py:365
  13.2 0.0 collective-permute-done.from_minus_ref.x_minus_ref
  13.2 0.0 collective-permute-done.1.from_plus_ref.x_plus_ref
  13.2 4.9 %all-to-all-done.refs_0_ = bf16[32,24,128]{2,1,0:T(8,128)(2,1)S(1)} async-done(((bf16[32,24,128]{2,1,0:T(8,128)(2,1)}), bf16[32,24,128]{2,1,0:T(8,128)(2,1)S(1)}, u32[]{:S(2)}, u32[]{:S(2)}) %all-to-all-start) | async-done | bytes 196640 | tf_op jit(solution)/shard_map/all_to_all | solution.py:45
  18.2 12.6 %waves.1 = bf16[32,24,128]{2,1,0:T(8,128)(2,1)} custom-call(bf16[32,24,128]{2,1,0:T(8,128)(2,1)S(1)} %all-to-all-done.refs_0_, bf16[512,24]{1,0:T(8,128)(2,1)S(1)} %get-tuple-element.59.refs_1_, f32[64,512]{1,0:T(8,128)S(1)} %get-tuple-element.60.refs_2_), custom_call_target="tpu_custom_call" | custom-call | flops 83886080 | bytes 1048576 | tf_op jit(solution)/shard_map/waves/pallas_call | solution.py:381
  30.7 3.0 %all-to-all-start.1 = ((bf16[32,24,128]{2,1,0:T(8,128)(2,1)}), bf16[32,24,128]{2,1,0:T(8,128)(2,1)S(1)}, u32[]{:S(2)}, u32[]{:S(2)}) async-start(bf16[32,24,128]{2,1,0:T(8,128)(2,1)} %waves.1), calls=%async_computation.1 | async-start | bytes 393216 | tf_op jit(solution)/shard_map/all_to_all | solution.py:45
  33.8 0.2 second_send.1
  34.0 1.8 %collective-permute-start.2 = (bf16[32,128]{1,0:T(8,128)(2,1)S(1)}, bf16[32,128]{1,0:T(8,128)(2,1)S(1)}, u32[]{:S(2)}, u32[]{:S(2)}) collective-permute-start(bf16[32,128]{1,0:T(8,128)(2,1)S(1)} %get-tuple-element.71), channel_id=1, source_target_pairs={{7,0},{0,1},{1,2},{2,3},{3,4},{4,5},{5,6},{6,7},{15,8},{8,9},{9,10... | collective-permute-start | bytes 24584 | tf_op jit(solution)/shard_map/ppermute | solution.py:37
  35.7 3.0 %collective-permute-start.3 = (bf16[32,128]{1,0:T(8,128)(2,1)S(1)}, bf16[32,128]{1,0:T(8,128)(2,1)S(1)}, u32[]{:S(2)}, u32[]{:S(2)}) collective-permute-start(bf16[32,128]{1,0:T(8,128)(2,1)S(1)} %get-tuple-element.72), channel_id=1, source_target_pairs={{1,0},{2,1},{3,2},{4,3},{5,4},{6,5},{7,6},{0,7},{9,8},{10,9},{11,1... | collective-permute-start | bytes 24584 | tf_op jit(solution)/shard_map/ppermute | solution.py:37
  38.7 2.3 %filters.1.filters_ref = f32[64,128,128]{2,1,0:T(8,128)S(1)} custom-call(s32[1,128]{1,0:T(1,128)S(1)} %get-tuple-element.66.count_ref, f32[64,128]{1,0:T(8,128)S(1)} %get-tuple-element.67.distances_ref, bf16[20,128]{1,0:T(8,128)(2,1)S(1)} %get-tuple-element.68.w_in_ref, bf16[128,128]{1,0:T(8,128)(2,1)S(1)} %get-tuple-element.69.w_out_ref), custom_call_target="tpu_custom_call" | custom-call | flops 268435456 | bytes 1048576 | tf_op jit(solution)/shard_map/filters/pallas_call | solution.py:408
  41.0 1.7 %collective-permute-done.2.y_minus_ref = bf16[32,128]{1,0:T(8,128)(2,1)S(1)} collective-permute-done((bf16[32,128]{1,0:T(8,128)(2,1)S(1)}, bf16[32,128]{1,0:T(8,128)(2,1)S(1)}, u32[]{:S(2)}, u32[]{:S(2)}) %collective-permute-start.2) | collective-permute-done | bytes 8224 | tf_op jit(solution)/shard_map/ppermute | solution.py:37
  42.7 0.0 collective-permute-done.3.y_plus_ref
  42.7 1.0 %messages.1.refs_0_ = f32[128,128]{1,0:T(8,128)S(1)} custom-call(bf16[128,128]{1,0:T(8,128)(2,1)S(1)} %get-tuple-element.55.features_ref, bf16[32,128]{1,0:T(8,128)(2,1)S(1)} %collective-permute-done.from_minus_ref.x_minus_ref, bf16[32,128]{1,0:T(8,128)(2,1)S(1)} %collective-permute-done.1.from_plus_ref.x_plus_ref, ...), custom_call_target="tpu_custom_call" | custom-call | flops 536870912 | bytes 1048576 | tf_op jit(solution)/shard_map/messages/pallas_call | solution.py:419
  43.7 0.0 all-to-all-done.1.refs_1_
  43.7 0.9 %final.1 = (bf16[128,128]{1,0:T(8,128)(2,1)}, f32[3,128]{1,0:T(4,128)}) custom-call(f32[128,128]{1,0:T(8,128)S(1)} %messages.1.refs_0_, bf16[32,24,128]{2,1,0:T(8,128)(2,1)S(1)} %all-to-all-done.1.refs_1_, f32[16,128]{1,0:T(8,128)S(1)} %get-tuple-element.79.refs_2_), custom_call_target="tpu_custom_call" | custom-call | tf_op jit(solution)/shard_map/final/pallas_call | solution.py:430
Async XLA Ops:
  2.3 15.9 %all-to-all-start = ((bf16[32,24,128]{2,1,0:T(8,128)(2,1)}), bf16[32,24,128]{2,1,0:T(8,128)(2,1)S(1)}, u32[]{:S(2)}, u32[]{:S(2)}) async-start(bf16[32,24,128]{2,1,0:T(8,128)(2,1)} %get-tuple-element.41), calls=%async_computation | async-start | bytes 393216 | tf_op jit(solution)/shard_map/all_to_all | solution.py:45
  9.6 3.6 %collective-permute-start = (bf16[32,128]{1,0:T(8,128)(2,1)S(1)}, bf16[32,128]{1,0:T(8,128)(2,1)S(1)}, u32[]{:S(2)}, u32[]{:S(2)}) collective-permute-start(bf16[32,128]{1,0:T(8,128)(2,1)S(1)} %get-tuple-element.42), channel_id=1, source_target_pairs={{24,0},{0,8},{8,16},{16,24},{25,1},{1,9},{9,17},{17,25},{26,2},{2,... | collective-permute-start | bytes 24584 | tf_op jit(solution)/shard_map/ppermute | solution.py:37
  9.9 3.3 %collective-permute-start.1 = (bf16[32,128]{1,0:T(8,128)(2,1)S(1)}, bf16[32,128]{1,0:T(8,128)(2,1)S(1)}, u32[]{:S(2)}, u32[]{:S(2)}) collective-permute-start(bf16[32,128]{1,0:T(8,128)(2,1)S(1)} %get-tuple-element.43), channel_id=1, source_target_pairs={{8,0},{16,8},{24,16},{0,24},{9,1},{17,9},{25,17},{1,25},{10,2},{18... | collective-permute-start | bytes 24584 | tf_op jit(solution)/shard_map/ppermute | solution.py:37
  30.7 13.0 %all-to-all-start.1 = ((bf16[32,24,128]{2,1,0:T(8,128)(2,1)}), bf16[32,24,128]{2,1,0:T(8,128)(2,1)S(1)}, u32[]{:S(2)}, u32[]{:S(2)}) async-start(bf16[32,24,128]{2,1,0:T(8,128)(2,1)} %waves.1), calls=%async_computation.1 | async-start | bytes 393216 | tf_op jit(solution)/shard_map/all_to_all | solution.py:45
  34.0 8.8 %collective-permute-start.2 = (bf16[32,128]{1,0:T(8,128)(2,1)S(1)}, bf16[32,128]{1,0:T(8,128)(2,1)S(1)}, u32[]{:S(2)}, u32[]{:S(2)}) collective-permute-start(bf16[32,128]{1,0:T(8,128)(2,1)S(1)} %get-tuple-element.71), channel_id=1, source_target_pairs={{7,0},{0,1},{1,2},{2,3},{3,4},{4,5},{5,6},{6,7},{15,8},{8,9},{9,10... | collective-permute-start | bytes 24584 | tf_op jit(solution)/shard_map/ppermute | solution.py:37
  35.7 7.0 %collective-permute-start.3 = (bf16[32,128]{1,0:T(8,128)(2,1)S(1)}, bf16[32,128]{1,0:T(8,128)(2,1)S(1)}, u32[]{:S(2)}, u32[]{:S(2)}) collective-permute-start(bf16[32,128]{1,0:T(8,128)(2,1)S(1)} %get-tuple-element.72), channel_id=1, source_target_pairs={{1,0},{2,1},{3,2},{4,3},{5,4},{6,5},{7,6},{0,7},{9,8},{10,9},{11,1... | collective-permute-start | bytes 24584 | tf_op jit(solution)/shard_map/ppermute | solution.py:37

commit v2 on v1

--- a/solution.py
+++ b/solution.py
@@ -168,15 +168,15 @@
     turns_ref[...] = dot(integers_ref[...], joined_ref[...], ((1,), (0,)))
 
     def step(index, unused):
-        for part in range(2):
-            lanes = pl.ds(pl.multiple_of((2 * index + part) * own, own), own)
+        for part in range(8):
+            lanes = pl.ds(pl.multiple_of((8 * index + part) * own, own), own)
             for first in range(0, count, chunk):
                 cosine, sine = waves_of(turns_ref[first : first + chunk, lanes])
                 waves_ref[first : first + chunk, lanes] = cosine.astype(bf16)
                 waves_ref[count + first : count + first + chunk, lanes] = sine.astype(bf16)
         return unused
 
-    lax.fori_loop(0, devices // 2, step, 0)
+    lax.fori_loop(0, devices // 8, step, 0)
     return [
         dot(waves_ref[wave * count : (wave + 1) * count, :], weights_ref[...], ((1,), (1,))) for wave in range(2)
     ]
@@ -193,7 +193,7 @@
         return waves_ref[wave * count : (wave + 1) * count, lanes]
 
     def step(turn, unused):
-        indices = (2 * turn, 2 * turn + 1)
+        indices = [4 * turn + i for i in range(4)]
         fields_of = [
             sum(dot(coefficients_ref[wave], waves_at(index, wave), ((1,), (0,))) for wave in range(2))
             for index in indices
@@ -211,7 +211,7 @@
                 result_ref[per_tile * index + i] = result[:, i * own : (i + 1) * own].astype(result_ref.dtype)
         return unused
 
-    lax.fori_loop(0, devices // (2 * per_tile), step, 0)
+    lax.fori_loop(0, devices // (4 * per_tile), step, 0)
 
 
 def waves_kernel(channels, gathered_ref, integers_ref, factors_ref, result_ref, waves_ref, coefficients_ref, *scratch):
@@ -271,33 +271,44 @@
     lax.fori_loop(0, slots // filter_group, step, 0)
 
 
-def messages_kernel(
-    features_ref, x_minus_ref, x_plus_ref, y_minus_ref, y_plus_ref, neighbours_ref, filters_ref, w_update_ref,
-    result_ref, table_ref,
-):
+def neighbour_sum(parts, first, neighbours_ref, filters_ref, table_ref, total):
     slots, own = neighbours_ref.shape
-    width = features_ref.shape[1]
-    first = 0
-    for part in (features_ref, x_minus_ref, x_plus_ref, y_minus_ref, y_plus_ref):
-        table_ref[first : first + part.shape[0], :] = part[...].astype(f32)
-        first += part.shape[0]
+    count = table_ref.shape[0]
+    filled = 0
+    for part in parts:
+        table_ref[filled : filled + part.shape[0], :] = part[...].astype(f32)
+        filled += part.shape[0]
     table = table_ref[...].T.astype(bf16)
-    row_ids = lax.broadcasted_iota(jnp.int32, (first, own), 0).astype(f32).astype(bf16)
-    ones, zeros = jnp.ones((first, own), bf16), jnp.zeros((first, own), bf16)
-
+    row_ids = (lax.broadcasted_iota(jnp.int32, (count, own), 0) + first).astype(f32).astype(bf16)
+    ones, zeros = jnp.ones((count, own), bf16), jnp.zeros((count, own), bf16)
     ids = neighbours_ref[...].astype(f32)
     rows = []
     for pair in range(0, slots, 2):
         chosen = []
         for slot in (pair, pair + 1):
             wanted = jnp.broadcast_to(ids[slot : slot + 1], (16, own)).astype(bf16)
-            wanted = jnp.concatenate([wanted] * (first // 16), axis=0)
+            wanted = jnp.concatenate([wanted] * (count // 16), axis=0)
             chosen.append(jnp.where(row_ids == wanted, ones, zeros))
         rows.append(dot(table, jnp.concatenate(chosen, axis=1), ((1,), (0,))))
-    total = jnp.zeros((width, own), f32)
     for slot in range(slots):
         lanes = slice(slot % 2 * own, (slot % 2 + 1) * own)
         total = total + rows[slot // 2][:, lanes] * filters_ref[slot]
+    return total
+
+
+def inner_kernel(features_ref, x_minus_ref, x_plus_ref, neighbours_ref, filters_ref, total_ref, table_ref):
+    parts = (features_ref, x_minus_ref, x_plus_ref)
+    total_ref[...] = neighbour_sum(
+        parts, 0, neighbours_ref, filters_ref, table_ref, jnp.zeros(total_ref.shape, f32)
+    )
+
+
+def outer_kernel(
+    first, y_minus_ref, y_plus_ref, neighbours_ref, filters_ref, total_ref, features_ref, w_update_ref,
+    result_ref, table_ref,
+):
+    parts = (y_minus_ref, y_plus_ref)
+    total = neighbour_sum(parts, first, neighbours_ref, filters_ref, table_ref, total_ref[...])
     update = dot(total.T.astype(bf16), w_update_ref[...], ((1,), (0,)))
     result_ref[...] = features_ref[...].astype(f32) + update
 
@@ -370,11 +381,17 @@
         compiler_params=small,
         name="hold",
     )(*[pltpu.with_memory_space_constraint(array, pltpu.HBM) for array in later])
-    gathered, x_minus, x_plus, integers, factors, later = lax.optimization_barrier(
-        (over_devices(copies), x_minus, x_plus, integers, factors, later)
+    y_minus, y_plus = pl.pallas_call(
+        second_send_kernel,
+        out_shape=(struct((ghosts, width), bf16), struct((ghosts, width), bf16)),
+        compiler_params=small,
+        name="second_send",
+    )(later[0], x_minus, x_plus, later[1])
+    gathered, x_minus, x_plus, y_minus, y_plus, integers, factors, later = lax.optimization_barrier(
+        (over_devices(copies), x_minus, x_plus, y_minus, y_plus, integers, factors, later)
     )
     (
-        features, send_along_y, neighbours, neighbour_count, distances,
+        features, _, neighbours, neighbour_count, distances,
         w_filter_in, filter_output_weight, update_weight, w_long,
     ) = later
     held_bytes = devices * own * (8 * count + 2 * (128 + 2 * payload_rows + result_rows))
@@ -392,15 +409,9 @@
         cost_estimate=pl.CostEstimate(flops=40 * count * devices * own, bytes_accessed=1 << 20, transcendentals=0),
         name="waves",
     )(gathered, integers, factors)
-    partial, x_minus, x_plus = lax.optimization_barrier((partial, x_minus, x_plus))
+    partial, x_minus, y_minus, y_plus = lax.optimization_barrier((partial, x_minus, y_minus, y_plus))
     received = over_devices(partial)
 
-    y_minus, y_plus = pl.pallas_call(
-        second_send_kernel,
-        out_shape=(struct((ghosts, width), bf16), struct((ghosts, width), bf16)),
-        compiler_params=small,
-        name="second_send",
-    )(features, x_minus, x_plus, send_along_y)
     y_minus = passed_along(y_minus, "gy", 1)
     y_plus = passed_along(y_plus, "gy", -1)
     slots = neighbours.shape[0]
@@ -415,17 +426,28 @@
         ),
         name="filters",
     )(neighbour_count, distances, w_filter_in, filter_output_weight)
-    filters, y_minus, y_plus = lax.optimization_barrier((filters, y_minus, y_plus))
+    inner_rows = own + 2 * ghosts
+    inner = pl.pallas_call(
+        inner_kernel,
+        out_shape=struct((width, own), f32),
+        scratch_shapes=[pltpu.VMEM((inner_rows, width), f32)],
+        compiler_params=small,
+        cost_estimate=pl.CostEstimate(
+            flops=2 * slots * own * width * inner_rows, bytes_accessed=1 << 20, transcendentals=0
+        ),
+        name="inner",
+    )(features, x_minus, x_plus, neighbours, filters)
+    inner, y_minus, y_plus = lax.optimization_barrier((inner, y_minus, y_plus))
     base = pl.pallas_call(
-        messages_kernel,
+        lambda *refs: outer_kernel(inner_rows, *refs),
         out_shape=struct((own, width), f32),
-        scratch_shapes=[pltpu.VMEM((own + 4 * ghosts, width), f32)],
+        scratch_shapes=[pltpu.VMEM((2 * ghosts, width), f32)],
         compiler_params=small,
         cost_estimate=pl.CostEstimate(
-            flops=2 * slots * own * width * 256, bytes_accessed=1 << 20, transcendentals=0
+            flops=4 * slots * own * width * ghosts, bytes_accessed=1 << 20, transcendentals=0
         ),
-        name="messages",
-    )(features, x_minus, x_plus, y_minus, y_plus, neighbours, filters, update_weight)
+        name="outer",
+    )(y_minus, y_plus, neighbours, filters, inner, features, update_weight)
 
     updated, forces = pl.pallas_call(
         lambda *refs: final_kernel(channels, *refs),

time: 45 us -> 44.5 us (0.989)
  waiting for transfers between devices: 6.63 us -> 5.84 us
    pallas_call x1 -> x2, Pallas kernels: 0.96 us -> 1.72 us  [the longest x1 0.97 us: per_device(): pl.pallas_call(lambda *refs: outer_kernel(inner_rows, *refs), out_shape=s...]
    ppermute x4, waiting for transfers between devices: 1.72 us -> 1.12 us  [passed_along(): return lax.ppermute(block, axis, route)]
    pallas_call x1, Pallas kernels: 12.6 us -> 12 us  [per_device(): pl.pallas_call(lambda *refs: waves_kernel(channels, *refs), out_shape=str...]
  transfers between devices with their start and end apart: 6 -> 6, of which waited for: 2 -> 2; matrix products, arithmetic and copies ran while one was open for 0% -> 0% of each run, Pallas kernels for 12% -> 14%
where the time goes in v2:
time: 44.5 us; the launch traced here: 44.1 us
  Pallas kernels  20.6 us (46%)
  starting transfers between devices  16.9 us (38%)
  waiting for transfers between devices  5.84 us (13%)
  between operations  0.71 us (2%)
    pallas_call x1, Pallas kernels, per_device(): pl.pallas_call(lambda *refs: waves_kernel(channels, *refs), out_shape=str...  12 us
    all_to_all x2, starting transfers between devices, over_devices(): return lax.all_to_all(blocks, ('gx', 'gy'), 0, 0, tiled=True)  10.4 us
    ppermute x4, starting transfers between devices, passed_along(): return lax.ppermute(block, axis, route)  6.57 us
    all_to_all x2, waiting for transfers between devices, over_devices(): return lax.all_to_all(blocks, ('gx', 'gy'), 0, 0, tiled=True)  4.72 us
    pallas_call x1, Pallas kernels, per_device(): pl.pallas_call(filters_kernel, out_shape=struct((slots, width, own), f32)...  2.31 us
    pallas_call x1, Pallas kernels, per_device(): pl.pallas_call(send_kernel, out_shape=(struct((devices, payload_rows, own...  1.65 us
    ppermute x4, waiting for transfers between devices, passed_along(): return lax.ppermute(block, axis, route)  1.12 us
    pallas_call x1, Pallas kernels, per_device(): pl.pallas_call(lambda *refs: outer_kernel(inner_rows, *refs), out_shape=s...  0.97 us
  transfers between devices with their start and end apart: 6, of which 2 were waited for; matrix products, arithmetic and copies ran while one was open for 0% of the time, Pallas kernels for 14%

profile of v2, /device:TPU:0, one launch (start us, length us, event | category | flops | bytes accessed | tf_op | source)
XLA Modules:
  0.0 44.1 jit_solution(18373547232507297403)
XLA Ops:
  0.6 1.7 %send.1 = (bf16[32,24,128]{2,1,0:T(8,128)(2,1)}, bf16[32,128]{1,0:T(8,128)(2,1)S(1)}, bf16[32,128]{1,0:T(8,128)(2,1)S(1)}) custom-call(bf16[128,128]{1,0:T(8,128)(2,1)} %refs_0_.4, f32[3,128]{1,0:T(4,128)} %refs_1_.2, bf16[16,128]{1,0:T(8,128)(2,1)} %bitcast.3, s32[2,32]{1,0:T(2,128)} %refs_3_.1), custom_call_target="tpu_custom_call" | custom-call | tf_op jit(solution)/shard_map/send/pallas_call | solution.py:336
  2.3 7.3 %all-to-all-start = ((bf16[32,24,128]{2,1,0:T(8,128)(2,1)}), bf16[32,24,128]{2,1,0:T(8,128)(2,1)S(1)}, u32[]{:S(2)}, u32[]{:S(2)}) async-start(bf16[32,24,128]{2,1,0:T(8,128)(2,1)} %get-tuple-element.43), calls=%async_computation | async-start | bytes 393216 | tf_op jit(solution)/shard_map/all_to_all | solution.py:45
  9.6 0.3 collective-permute-start
  9.9 1.5 %collective-permute-start.1 = (bf16[32,128]{1,0:T(8,128)(2,1)S(1)}, bf16[32,128]{1,0:T(8,128)(2,1)S(1)}, u32[]{:S(2)}, u32[]{:S(2)}) collective-permute-start(bf16[32,128]{1,0:T(8,128)(2,1)S(1)} %get-tuple-element.45), channel_id=1, source_target_pairs={{8,0},{16,8},{24,16},{0,24},{9,1},{17,9},{25,17},{1,25},{10,2},{18... | collective-permute-start | bytes 24584 | tf_op jit(solution)/shard_map/ppermute | solution.py:37
  11.4 0.8 %factors.1 = (bf16[512,24]{1,0:T(8,128)(2,1)S(1)}, f32[64,512]{1,0:T(8,128)S(1)}) custom-call(s32[3,16384]{1,0:T(4,128)} %refs_0_.5, f32[1,16]{1,0:T(1,128)} %bitcast.4), custom_call_target="tpu_custom_call" | custom-call | tf_op jit(solution)/shard_map/factors/pallas_call | solution.py:359
  12.3 1.0 %hold.1 = (bf16[128,128]{1,0:T(8,128)(2,1)S(1)}, s32[2,32]{1,0:T(2,128)S(1)}, s32[64,128]{1,0:T(8,128)S(1)}, s32[1,128]{1,0:T(1,128)S(1)}, f32[64,128]{1,0:T(8,1...) custom-call(bf16[128,128]{1,0:T(8,128)(2,1)} %refs_0_.4, ...), custom_call_target="tpu_custom_call" | custom-call | tf_op jit(solution)/shard_map/hold/pallas_call | solution.py:376
  13.2 0.0 collective-permute-done.from_minus_ref.x_minus_ref
  13.2 0.0 collective-permute-done.1.from_plus_ref.x_plus_ref
  13.2 0.2 second_send.1
  13.4 4.7 %all-to-all-done.refs_0_ = bf16[32,24,128]{2,1,0:T(8,128)(2,1)S(1)} async-done(((bf16[32,24,128]{2,1,0:T(8,128)(2,1)}), bf16[32,24,128]{2,1,0:T(8,128)(2,1)S(1)}, u32[]{:S(2)}, u32[]{:S(2)}) %all-to-all-start) | async-done | bytes 196640 | tf_op jit(solution)/shard_map/all_to_all | solution.py:45
  18.2 12.0 %waves.1 = bf16[32,24,128]{2,1,0:T(8,128)(2,1)} custom-call(bf16[32,24,128]{2,1,0:T(8,128)(2,1)S(1)} %all-to-all-done.refs_0_, bf16[512,24]{1,0:T(8,128)(2,1)S(1)} %get-tuple-element.63.refs_1_, f32[64,512]{1,0:T(8,128)S(1)} %get-tuple-element.64.refs_2_), custom_call_target="tpu_custom_call" | custom-call | flops 83886080 | bytes 1048576 | tf_op jit(solution)/shard_map/waves/pallas_call | solution.py:398
  30.1 3.0 %all-to-all-start.1 = ((bf16[32,24,128]{2,1,0:T(8,128)(2,1)}), bf16[32,24,128]{2,1,0:T(8,128)(2,1)S(1)}, u32[]{:S(2)}, u32[]{:S(2)}) async-start(bf16[32,24,128]{2,1,0:T(8,128)(2,1)} %waves.1), calls=%async_computation.1 | async-start | bytes 393216 | tf_op jit(solution)/shard_map/all_to_all | solution.py:45
  33.2 1.8 %collective-permute-start.2 = (bf16[32,128]{1,0:T(8,128)(2,1)S(1)}, bf16[32,128]{1,0:T(8,128)(2,1)S(1)}, u32[]{:S(2)}, u32[]{:S(2)}) collective-permute-start(bf16[32,128]{1,0:T(8,128)(2,1)S(1)} %get-tuple-element.76), channel_id=1, source_target_pairs={{7,0},{0,1},{1,2},{2,3},{3,4},{4,5},{5,6},{6,7},{15,8},{8,9},{9,10... | collective-permute-start | bytes 24584 | tf_op jit(solution)/shard_map/ppermute | solution.py:37
  35.0 3.0 %collective-permute-start.3 = (bf16[32,128]{1,0:T(8,128)(2,1)S(1)}, bf16[32,128]{1,0:T(8,128)(2,1)S(1)}, u32[]{:S(2)}, u32[]{:S(2)}) collective-permute-start(bf16[32,128]{1,0:T(8,128)(2,1)S(1)} %get-tuple-element.77), channel_id=1, source_target_pairs={{1,0},{2,1},{3,2},{4,3},{5,4},{6,5},{7,6},{0,7},{9,8},{10,9},{11,1... | collective-permute-start | bytes 24584 | tf_op jit(solution)/shard_map/ppermute | solution.py:37
  38.0 2.3 %filters.1.filters_ref.refs_3_ = f32[64,128,128]{2,1,0:T(8,128)S(1)} custom-call(s32[1,128]{1,0:T(1,128)S(1)} %get-tuple-element.72.count_ref, f32[64,128]{1,0:T(8,128)S(1)} %get-tuple-element.73.distances_ref, bf16[20,128]{1,0:T(8,128)(2,1)S(1)} %get-tuple-element.74.w_in_ref, bf16[128,128]{1,0:T(8,128)(2,1)S(1)} %get-tuple-element.75.w_out_ref), custom_call_target="tpu_custom_call" | custom-call | flops 268435456 | bytes 1048576 | tf_op jit(solution)/shard_map/filters/pallas_call | solution.py:419
  40.3 0.8 %inner.1.refs_4_ = f32[128,128]{1,0:T(8,128)S(1)} custom-call(bf16[128,128]{1,0:T(8,128)(2,1)S(1)} %get-tuple-element.59.features_ref.refs_5_, bf16[32,128]{1,0:T(8,128)(2,1)S(1)} %collective-permute-done.from_minus_ref.x_minus_ref, bf16[32,128]{1,0:T(8,128)(2,1)S(1)} %collective-permute-done.1.from_plus_ref.x_plus_ref, ...), custom_call_target="tpu_custom_call" | custom-call | flops 402653184 | bytes 1048576 | tf_op jit(solution)/shard_map/inner/pallas_call | solution.py:430
  41.1 1.1 %collective-permute-done.2.refs_0_ = bf16[32,128]{1,0:T(8,128)(2,1)S(1)} collective-permute-done((bf16[32,128]{1,0:T(8,128)(2,1)S(1)}, bf16[32,128]{1,0:T(8,128)(2,1)S(1)}, u32[]{:S(2)}, u32[]{:S(2)}) %collective-permute-start.2) | collective-permute-done | bytes 8224 | tf_op jit(solution)/shard_map/ppermute | solution.py:37
  42.2 0.0 collective-permute-done.3.refs_1_
  42.2 1.0 %outer.1.refs_0_ = f32[128,128]{1,0:T(8,128)S(1)} custom-call(bf16[32,128]{1,0:T(8,128)(2,1)S(1)} %collective-permute-done.2.refs_0_, bf16[32,128]{1,0:T(8,128)(2,1)S(1)} %collective-permute-done.3.refs_1_, s32[64,128]{1,0:T(8,128)S(1)} %get-tuple-element.71.neighbours_ref.refs_2_, f32[64,128,128]{2,1,0:T(8,128)S(1)} %filters.1.filters_ref.refs_3_, ...), custom_call_target="tpu_custom_call" | custom-call | flops 134217728 | bytes 1048576 | tf_op jit(solution)/shard_map/outer/pallas_call | solution.py:441
  43.1 0.0 all-to-all-done.1.refs_1_
  43.1 0.9 %final.1 = (bf16[128,128]{1,0:T(8,128)(2,1)}, f32[3,128]{1,0:T(4,128)}) custom-call(f32[128,128]{1,0:T(8,128)S(1)} %outer.1.refs_0_, bf16[32,24,128]{2,1,0:T(8,128)(2,1)S(1)} %all-to-all-done.1.refs_1_, f32[16,128]{1,0:T(8,128)S(1)} %get-tuple-element.83.refs_2_), custom_call_target="tpu_custom_call" | custom-call | tf_op jit(solution)/shard_map/final/pallas_call | solution.py:452
Async XLA Ops:
  2.3 15.9 %all-to-all-start = ((bf16[32,24,128]{2,1,0:T(8,128)(2,1)}), bf16[32,24,128]{2,1,0:T(8,128)(2,1)S(1)}, u32[]{:S(2)}, u32[]{:S(2)}) async-start(bf16[32,24,128]{2,1,0:T(8,128)(2,1)} %get-tuple-element.43), calls=%async_computation | async-start | bytes 393216 | tf_op jit(solution)/shard_map/all_to_all | solution.py:45
  9.6 3.6 %collective-permute-start = (bf16[32,128]{1,0:T(8,128)(2,1)S(1)}, bf16[32,128]{1,0:T(8,128)(2,1)S(1)}, u32[]{:S(2)}, u32[]{:S(2)}) collective-permute-start(bf16[32,128]{1,0:T(8,128)(2,1)S(1)} %get-tuple-element.44), channel_id=1, source_target_pairs={{24,0},{0,8},{8,16},{16,24},{25,1},{1,9},{9,17},{17,25},{26,2},{2,... | collective-permute-start | bytes 24584 | tf_op jit(solution)/shard_map/ppermute | solution.py:37
  9.9 3.3 %collective-permute-start.1 = (bf16[32,128]{1,0:T(8,128)(2,1)S(1)}, bf16[32,128]{1,0:T(8,128)(2,1)S(1)}, u32[]{:S(2)}, u32[]{:S(2)}) collective-permute-start(bf16[32,128]{1,0:T(8,128)(2,1)S(1)} %get-tuple-element.45), channel_id=1, source_target_pairs={{8,0},{16,8},{24,16},{0,24},{9,1},{17,9},{25,17},{1,25},{10,2},{18... | collective-permute-start | bytes 24584 | tf_op jit(solution)/shard_map/ppermute | solution.py:37
  30.1 13.0 %all-to-all-start.1 = ((bf16[32,24,128]{2,1,0:T(8,128)(2,1)}), bf16[32,24,128]{2,1,0:T(8,128)(2,1)S(1)}, u32[]{:S(2)}, u32[]{:S(2)}) async-start(bf16[32,24,128]{2,1,0:T(8,128)(2,1)} %waves.1), calls=%async_computation.1 | async-start | bytes 393216 | tf_op jit(solution)/shard_map/all_to_all | solution.py:45
  33.2 9.0 %collective-permute-start.2 = (bf16[32,128]{1,0:T(8,128)(2,1)S(1)}, bf16[32,128]{1,0:T(8,128)(2,1)S(1)}, u32[]{:S(2)}, u32[]{:S(2)}) collective-permute-start(bf16[32,128]{1,0:T(8,128)(2,1)S(1)} %get-tuple-element.76), channel_id=1, source_target_pairs={{7,0},{0,1},{1,2},{2,3},{3,4},{4,5},{5,6},{6,7},{15,8},{8,9},{9,10... | collective-permute-start | bytes 24584 | tf_op jit(solution)/shard_map/ppermute | solution.py:37
  35.0 7.1 %collective-permute-start.3 = (bf16[32,128]{1,0:T(8,128)(2,1)S(1)}, bf16[32,128]{1,0:T(8,128)(2,1)S(1)}, u32[]{:S(2)}, u32[]{:S(2)}) collective-permute-start(bf16[32,128]{1,0:T(8,128)(2,1)S(1)} %get-tuple-element.77), channel_id=1, source_target_pairs={{1,0},{2,1},{3,2},{4,3},{5,4},{6,5},{7,6},{0,7},{9,8},{10,9},{11,1... | collective-permute-start | bytes 24584 | tf_op jit(solution)/shard_map/ppermute | solution.py:37

commit v3 on v2

--- a/solution.py
+++ b/solution.py
@@ -155,7 +155,6 @@
     count = integers_ref.shape[0]
     chunk = min(count, 128)
     weights_ref[channels : 2 * channels, :] = jnp.ones((channels, devices * own), bf16)
-    weights_ref[2 * channels :, :] = jnp.zeros((128 - 2 * channels, devices * own), bf16)
 
     def join(index, unused):
         lanes = pl.ds(pl.multiple_of(index * own, own), own)
@@ -177,9 +176,8 @@
         return unused
 
     lax.fori_loop(0, devices // 8, step, 0)
-    return [
-        dot(waves_ref[wave * count : (wave + 1) * count, :], weights_ref[...], ((1,), (1,))) for wave in range(2)
-    ]
+    sums = dot(waves_ref[...], weights_ref[...], ((1,), (1,)))
+    return [sums[:count], sums[count:]]
 
 
 def put_fields(channels, atoms, blocks_ref, waves_ref, coefficients_ref, mean, result_ref):
@@ -394,7 +392,7 @@
         features, _, neighbours, neighbour_count, distances,
         w_filter_in, filter_output_weight, update_weight, w_long,
     ) = later
-    held_bytes = devices * own * (8 * count + 2 * (128 + 2 * payload_rows + result_rows))
+    held_bytes = devices * own * (8 * count + 2 * (2 * channels + 2 * payload_rows + result_rows))
     partial = pl.pallas_call(
         lambda *refs: waves_kernel(channels, *refs),
         out_shape=struct((devices, result_rows, own), bf16),
@@ -402,7 +400,7 @@
             pltpu.VMEM((2 * count, devices * own), bf16),
             pltpu.VMEM((2, 4 * channels, count), bf16),
             pltpu.VMEM((payload_rows, devices * own), bf16),
-            pltpu.VMEM((128, devices * own), bf16),
+            pltpu.VMEM((2 * channels, devices * own), bf16),
             pltpu.VMEM((count, devices * own), f32),
         ],
         compiler_params=pltpu.CompilerParams(vmem_limit_bytes=held_bytes + 8 * 1024 * 1024),

time: 44.5 us -> 44.4 us (level)
  no operation moved by 1% of the time
where the time goes in v3:
time: 44.4 us; the launch traced here: 44 us
  Pallas kernels  20.5 us (46%)
  starting transfers between devices  16.9 us (38%)
  waiting for transfers between devices  5.83 us (13%)
  between operations  0.71 us (2%)
    pallas_call x1, Pallas kernels, per_device(): pl.pallas_call(lambda *refs: waves_kernel(channels, *refs), out_shape=str...  11.9 us
    all_to_all x2, starting transfers between devices, over_devices(): return lax.all_to_all(blocks, ('gx', 'gy'), 0, 0, tiled=True)  10.3 us
    ppermute x4, starting transfers between devices, passed_along(): return lax.ppermute(block, axis, route)  6.57 us
    all_to_all x2, waiting for transfers between devices, over_devices(): return lax.all_to_all(blocks, ('gx', 'gy'), 0, 0, tiled=True)  4.72 us
    pallas_call x1, Pallas kernels, per_device(): pl.pallas_call(filters_kernel, out_shape=struct((slots, width, own), f32)...  2.32 us
    pallas_call x1, Pallas kernels, per_device(): pl.pallas_call(send_kernel, out_shape=(struct((devices, payload_rows, own...  1.65 us
    ppermute x4, waiting for transfers between devices, passed_along(): return lax.ppermute(block, axis, route)  1.11 us
    pallas_call x1, Pallas kernels, per_device(): pl.pallas_call(lambda *refs: outer_kernel(inner_rows, *refs), out_shape=s...  0.97 us
  transfers between devices with their start and end apart: 6, of which 2 were waited for; matrix products, arithmetic and copies ran while one was open for 0% of the time, Pallas kernels for 14%

profile of v3, /device:TPU:0, one launch (start us, length us, event | category | flops | bytes accessed | tf_op | source)
XLA Modules:
  0.0 44.0 jit_solution(13138423764996277066)
XLA Ops:
  0.6 1.7 %send.1 = (bf16[32,24,128]{2,1,0:T(8,128)(2,1)}, bf16[32,128]{1,0:T(8,128)(2,1)S(1)}, bf16[32,128]{1,0:T(8,128)(2,1)S(1)}) custom-call(bf16[128,128]{1,0:T(8,128)(2,1)} %refs_0_.4, f32[3,128]{1,0:T(4,128)} %refs_1_.2, bf16[16,128]{1,0:T(8,128)(2,1)} %bitcast.3, s32[2,32]{1,0:T(2,128)} %refs_3_.1), custom_call_target="tpu_custom_call" | custom-call | tf_op jit(solution)/shard_map/send/pallas_call | solution.py:334
  2.3 7.3 %all-to-all-start = ((bf16[32,24,128]{2,1,0:T(8,128)(2,1)}), bf16[32,24,128]{2,1,0:T(8,128)(2,1)S(1)}, u32[]{:S(2)}, u32[]{:S(2)}) async-start(bf16[32,24,128]{2,1,0:T(8,128)(2,1)} %get-tuple-element.43), calls=%async_computation | async-start | bytes 393216 | tf_op jit(solution)/shard_map/all_to_all | solution.py:45
  9.6 0.3 collective-permute-start
  9.9 1.5 %collective-permute-start.1 = (bf16[32,128]{1,0:T(8,128)(2,1)S(1)}, bf16[32,128]{1,0:T(8,128)(2,1)S(1)}, u32[]{:S(2)}, u32[]{:S(2)}) collective-permute-start(bf16[32,128]{1,0:T(8,128)(2,1)S(1)} %get-tuple-element.45), channel_id=1, source_target_pairs={{8,0},{16,8},{24,16},{0,24},{9,1},{17,9},{25,17},{1,25},{10,2},{18... | collective-permute-start | bytes 24584 | tf_op jit(solution)/shard_map/ppermute | solution.py:37
  11.4 0.8 %factors.1 = (bf16[512,24]{1,0:T(8,128)(2,1)S(1)}, f32[64,512]{1,0:T(8,128)S(1)}) custom-call(s32[3,16384]{1,0:T(4,128)} %refs_0_.5, f32[1,16]{1,0:T(1,128)} %bitcast.4), custom_call_target="tpu_custom_call" | custom-call | tf_op jit(solution)/shard_map/factors/pallas_call | solution.py:357
  12.3 1.0 %hold.1 = (bf16[128,128]{1,0:T(8,128)(2,1)S(1)}, s32[2,32]{1,0:T(2,128)S(1)}, s32[64,128]{1,0:T(8,128)S(1)}, s32[1,128]{1,0:T(1,128)S(1)}, f32[64,128]{1,0:T(8,1...) custom-call(bf16[128,128]{1,0:T(8,128)(2,1)} %refs_0_.4, ...), custom_call_target="tpu_custom_call" | custom-call | tf_op jit(solution)/shard_map/hold/pallas_call | solution.py:374
  13.2 0.0 collective-permute-done.from_minus_ref.x_minus_ref
  13.2 0.0 collective-permute-done.1.from_plus_ref.x_plus_ref
  13.2 0.2 second_send.1
  13.4 4.7 %all-to-all-done.refs_0_ = bf16[32,24,128]{2,1,0:T(8,128)(2,1)S(1)} async-done(((bf16[32,24,128]{2,1,0:T(8,128)(2,1)}), bf16[32,24,128]{2,1,0:T(8,128)(2,1)S(1)}, u32[]{:S(2)}, u32[]{:S(2)}) %all-to-all-start) | async-done | bytes 196640 | tf_op jit(solution)/shard_map/all_to_all | solution.py:45
  18.2 11.9 %waves.1 = bf16[32,24,128]{2,1,0:T(8,128)(2,1)} custom-call(bf16[32,24,128]{2,1,0:T(8,128)(2,1)S(1)} %all-to-all-done.refs_0_, bf16[512,24]{1,0:T(8,128)(2,1)S(1)} %get-tuple-element.63.refs_1_, f32[64,512]{1,0:T(8,128)S(1)} %get-tuple-element.64.refs_2_), custom_call_target="tpu_custom_call" | custom-call | flops 83886080 | bytes 1048576 | tf_op jit(solution)/shard_map/waves/pallas_call | solution.py:396
  30.1 3.0 %all-to-all-start.1 = ((bf16[32,24,128]{2,1,0:T(8,128)(2,1)}), bf16[32,24,128]{2,1,0:T(8,128)(2,1)S(1)}, u32[]{:S(2)}, u32[]{:S(2)}) async-start(bf16[32,24,128]{2,1,0:T(8,128)(2,1)} %waves.1), calls=%async_computation.1 | async-start | bytes 393216 | tf_op jit(solution)/shard_map/all_to_all | solution.py:45
  33.1 1.8 %collective-permute-start.2 = (bf16[32,128]{1,0:T(8,128)(2,1)S(1)}, bf16[32,128]{1,0:T(8,128)(2,1)S(1)}, u32[]{:S(2)}, u32[]{:S(2)}) collective-permute-start(bf16[32,128]{1,0:T(8,128)(2,1)S(1)} %get-tuple-element.76), channel_id=1, source_target_pairs={{7,0},{0,1},{1,2},{2,3},{3,4},{4,5},{5,6},{6,7},{15,8},{8,9},{9,10... | collective-permute-start | bytes 24584 | tf_op jit(solution)/shard_map/ppermute | solution.py:37
  34.9 3.0 %collective-permute-start.3 = (bf16[32,128]{1,0:T(8,128)(2,1)S(1)}, bf16[32,128]{1,0:T(8,128)(2,1)S(1)}, u32[]{:S(2)}, u32[]{:S(2)}) collective-permute-start(bf16[32,128]{1,0:T(8,128)(2,1)S(1)} %get-tuple-element.77), channel_id=1, source_target_pairs={{1,0},{2,1},{3,2},{4,3},{5,4},{6,5},{7,6},{0,7},{9,8},{10,9},{11,1... | collective-permute-start | bytes 24584 | tf_op jit(solution)/shard_map/ppermute | solution.py:37
  37.9 2.3 %filters.1.filters_ref.refs_3_ = f32[64,128,128]{2,1,0:T(8,128)S(1)} custom-call(s32[1,128]{1,0:T(1,128)S(1)} %get-tuple-element.72.count_ref, f32[64,128]{1,0:T(8,128)S(1)} %get-tuple-element.73.distances_ref, bf16[20,128]{1,0:T(8,128)(2,1)S(1)} %get-tuple-element.74.w_in_ref, bf16[128,128]{1,0:T(8,128)(2,1)S(1)} %get-tuple-element.75.w_out_ref), custom_call_target="tpu_custom_call" | custom-call | flops 268435456 | bytes 1048576 | tf_op jit(solution)/shard_map/filters/pallas_call | solution.py:417
  40.2 0.8 %inner.1.refs_4_ = f32[128,128]{1,0:T(8,128)S(1)} custom-call(bf16[128,128]{1,0:T(8,128)(2,1)S(1)} %get-tuple-element.59.features_ref.refs_5_, bf16[32,128]{1,0:T(8,128)(2,1)S(1)} %collective-permute-done.from_minus_ref.x_minus_ref, bf16[32,128]{1,0:T(8,128)(2,1)S(1)} %collective-permute-done.1.from_plus_ref.x_plus_ref, ...), custom_call_target="tpu_custom_call" | custom-call | flops 402653184 | bytes 1048576 | tf_op jit(solution)/shard_map/inner/pallas_call | solution.py:428
  41.0 1.1 %collective-permute-done.2.refs_0_ = bf16[32,128]{1,0:T(8,128)(2,1)S(1)} collective-permute-done((bf16[32,128]{1,0:T(8,128)(2,1)S(1)}, bf16[32,128]{1,0:T(8,128)(2,1)S(1)}, u32[]{:S(2)}, u32[]{:S(2)}) %collective-permute-start.2) | collective-permute-done | bytes 8224 | tf_op jit(solution)/shard_map/ppermute | solution.py:37
  42.1 0.0 collective-permute-done.3.refs_1_
  42.1 1.0 %outer.1.refs_0_ = f32[128,128]{1,0:T(8,128)S(1)} custom-call(bf16[32,128]{1,0:T(8,128)(2,1)S(1)} %collective-permute-done.2.refs_0_, bf16[32,128]{1,0:T(8,128)(2,1)S(1)} %collective-permute-done.3.refs_1_, s32[64,128]{1,0:T(8,128)S(1)} %get-tuple-element.71.neighbours_ref.refs_2_, f32[64,128,128]{2,1,0:T(8,128)S(1)} %filters.1.filters_ref.refs_3_, ...), custom_call_target="tpu_custom_call" | custom-call | flops 134217728 | bytes 1048576 | tf_op jit(solution)/shard_map/outer/pallas_call | solution.py:439
  43.0 0.0 all-to-all-done.1.refs_1_
  43.0 0.9 %final.1 = (bf16[128,128]{1,0:T(8,128)(2,1)}, f32[3,128]{1,0:T(4,128)}) custom-call(f32[128,128]{1,0:T(8,128)S(1)} %outer.1.refs_0_, bf16[32,24,128]{2,1,0:T(8,128)(2,1)S(1)} %all-to-all-done.1.refs_1_, f32[16,128]{1,0:T(8,128)S(1)} %get-tuple-element.83.refs_2_), custom_call_target="tpu_custom_call" | custom-call | tf_op jit(solution)/shard_map/final/pallas_call | solution.py:450
Async XLA Ops:
  2.3 15.9 %all-to-all-start = ((bf16[32,24,128]{2,1,0:T(8,128)(2,1)}), bf16[32,24,128]{2,1,0:T(8,128)(2,1)S(1)}, u32[]{:S(2)}, u32[]{:S(2)}) async-start(bf16[32,24,128]{2,1,0:T(8,128)(2,1)} %get-tuple-element.43), calls=%async_computation | async-start | bytes 393216 | tf_op jit(solution)/shard_map/all_to_all | solution.py:45
  9.6 3.6 %collective-permute-start = (bf16[32,128]{1,0:T(8,128)(2,1)S(1)}, bf16[32,128]{1,0:T(8,128)(2,1)S(1)}, u32[]{:S(2)}, u32[]{:S(2)}) collective-permute-start(bf16[32,128]{1,0:T(8,128)(2,1)S(1)} %get-tuple-element.44), channel_id=1, source_target_pairs={{24,0},{0,8},{8,16},{16,24},{25,1},{1,9},{9,17},{17,25},{26,2},{2,... | collective-permute-start | bytes 24584 | tf_op jit(solution)/shard_map/ppermute | solution.py:37
  9.9 3.3 %collective-permute-start.1 = (bf16[32,128]{1,0:T(8,128)(2,1)S(1)}, bf16[32,128]{1,0:T(8,128)(2,1)S(1)}, u32[]{:S(2)}, u32[]{:S(2)}) collective-permute-start(bf16[32,128]{1,0:T(8,128)(2,1)S(1)} %get-tuple-element.45), channel_id=1, source_target_pairs={{8,0},{16,8},{24,16},{0,24},{9,1},{17,9},{25,17},{1,25},{10,2},{18... | collective-permute-start | bytes 24584 | tf_op jit(solution)/shard_map/ppermute | solution.py:37
  30.1 13.0 %all-to-all-start.1 = ((bf16[32,24,128]{2,1,0:T(8,128)(2,1)}), bf16[32,24,128]{2,1,0:T(8,128)(2,1)S(1)}, u32[]{:S(2)}, u32[]{:S(2)}) async-start(bf16[32,24,128]{2,1,0:T(8,128)(2,1)} %waves.1), calls=%async_computation.1 | async-start | bytes 393216 | tf_op jit(solution)/shard_map/all_to_all | solution.py:45
  33.1 9.0 %collective-permute-start.2 = (bf16[32,128]{1,0:T(8,128)(2,1)S(1)}, bf16[32,128]{1,0:T(8,128)(2,1)S(1)}, u32[]{:S(2)}, u32[]{:S(2)}) collective-permute-start(bf16[32,128]{1,0:T(8,128)(2,1)S(1)} %get-tuple-element.76), channel_id=1, source_target_pairs={{7,0},{0,1},{1,2},{2,3},{3,4},{4,5},{5,6},{6,7},{15,8},{8,9},{9,10... | collective-permute-start | bytes 24584 | tf_op jit(solution)/shard_map/ppermute | solution.py:37
  34.9 7.1 %collective-permute-start.3 = (bf16[32,128]{1,0:T(8,128)(2,1)S(1)}, bf16[32,128]{1,0:T(8,128)(2,1)S(1)}, u32[]{:S(2)}, u32[]{:S(2)}) collective-permute-start(bf16[32,128]{1,0:T(8,128)(2,1)S(1)} %get-tuple-element.77), channel_id=1, source_target_pairs={{1,0},{2,1},{3,2},{4,3},{5,4},{6,5},{7,6},{0,7},{9,8},{10,9},{11,1... | collective-permute-start | bytes 24584 | tf_op jit(solution)/shard_map/ppermute | solution.py:37
